TPU v7x, 512 devices: a whole 4x4x16 slice. The times are simulated.
512 devices in a mesh: rows: 64 (over x, z), mass: 8 (over y, core).
Axes of the slice: x: 4, y: 4, z: 16, core: 2. Of those that a mesh axis runs over, the one named last changes fastest.
Arguments:
- data: bfloat16 [98304, 4096], P('rows', 'mass'), may hold values from -3 to 580
- conc_init: float32 [64, 98304], P(None, 'rows'), may hold values from 0.05 to 3.5, as said below
- spec_init: float32 [64, 4096], P(None, 'mass'), may hold values from 0.05 to 3.5, as said below
Outputs:
- concentrations: float32 [64, 98304], P(None, 'rows')
- spectra: float32 [64, 4096], P(None, 'mass')
Inputs may be any that keep to these rules, and one draw needn't show every extreme that they name: `conc_init`: positive. `spec_init`: positive.
All inputs are finite; a program needn't handle non-finite values.
Results may differ from a plain program's by a relative error of at most 0.0017.
The roundings to bfloat16 on the way count: a program that leaves them out, or rounds other values in their place, can miss the bound.
Values sent between devices are 32-bit elements; how exact they have to be, the bound alone decides.
No kernel may reach another device: no remote copies, remote signals or barrier semaphores. Data moves between devices by JAX's collectives and lax.ppermute only.
A program may use at most 64 MiB of HBM per device.

v0:
```python
import jax
import jax.numpy as jnp
from jax import lax
from jax.sharding import PartitionSpec as P

ITERS = 2


def sweep_rows(factor, cross, gram):
    for index in range(gram.shape[0]):
        mixed = jnp.dot(gram[index], factor, precision=lax.Precision.HIGHEST)
        updated = factor[index] + (cross[index] - mixed) / gram[index, index]
        factor = factor.at[index].set(jnp.maximum(updated, 0.0001))
    return factor


def body(data, conc_init, spec_init):
    concentrations = conc_init
    spectra = spec_init
    inner = (((1,), (1,)), ((), ()))
    for step in range(ITERS):
        spec_low = spectra.astype(jnp.bfloat16)
        conc_cross = lax.dot_general(spec_low, data, inner, preferred_element_type=jnp.float32)
        spec_gram = lax.dot_general(spectra, spectra, inner, precision=lax.Precision.HIGHEST)
        conc_cross, spec_gram = lax.psum((conc_cross, spec_gram), "mass")
        concentrations = sweep_rows(concentrations, conc_cross, spec_gram)
        conc_low = concentrations.astype(jnp.bfloat16)
        spec_cross = jnp.dot(conc_low, data, preferred_element_type=jnp.float32)
        conc_gram = lax.dot_general(
            concentrations, concentrations, inner, precision=lax.Precision.HIGHEST
        )
        spec_cross, conc_gram = lax.psum((spec_cross, conc_gram), "rows")
        spectra = sweep_rows(spectra, spec_cross, conc_gram)
    return (concentrations, spectra)


def solution(mesh):
    return jax.shard_map(
        body,
        mesh=mesh,
        in_specs=(P("rows", "mass"), P(None, "rows"), P(None, "mass")),
        out_specs=(P(None, "rows"), P(None, "mass")),
        check_vma=False,
    )
```

profile of v0, /device:TPU:24, one launch (start us, length us, event | category | flops | bytes accessed | tf_op | source)
XLA Modules:
  0.0 1700.4 jit_solution(16725867303801387858)
XLA Ops:
  7.2 1.0 copy.268
  9.2 1.3 fusion.6
  10.9 24.7 %psum.57 = f32[64,64]{1,0:T(8,128)S(1)} all-reduce(f32[64,64]{1,0:T(8,128)S(1)} %fusion.288), channel_id=1, replica_groups=mesh['rows'=64,'mass'=8] {'mass'}, use_global_device_ids=true, to_apply=%region_1.0 | all-reduce | flops 4096 | bytes 32768 | tf_op jit(solution)/shard_map/psum | solution.py:25
  38.8 49.9 %all-reduce.5.cloned.1.call-done = f32[64,1536]{1,0:T(8,128)} async-done(((f32[64,1536]{1,0:T(8,128)}), f32[64,1536]{1,0:T(8,128)}) %all-reduce.5.cloned.1.call-update) | async-done | bytes 393232 | tf_op jit(solution)/shard_map/psum | solution.py:25
  88.7 1.3 slice_reduce_fusion.242
  90.9 1.1 convolution_reduce_fusion.126
  106.0 1.0 convolution_reduce_fusion.118
  107.9 1.0 convolution_reduce_fusion.117
  109.7 1.0 convolution_reduce_fusion.116
  111.6 1.0 convolution_reduce_fusion.115
  113.5 1.0 convolution_reduce_fusion.114
  115.3 1.0 convolution_reduce_fusion.113
  117.1 1.0 convolution_reduce_fusion.112
  120.8 1.0 convolution_reduce_fusion.110
  122.7 1.0 convolution_reduce_fusion.109
  124.6 1.0 convolution_reduce_fusion.108
  126.4 1.0 convolution_reduce_fusion.107
  128.4 1.0 convolution_reduce_fusion.106
  130.3 1.0 convolution_reduce_fusion.105
  132.1 1.0 convolution_reduce_fusion.104
  135.9 1.0 convolution_reduce_fusion.102
  137.7 1.0 convolution_reduce_fusion.101
  139.8 1.0 convolution_reduce_fusion.100
  141.9 1.0 convolution_reduce_fusion.99
  143.8 1.0 convolution_reduce_fusion.98
  145.7 1.0 convolution_reduce_fusion.97
  147.6 1.0 convolution_reduce_fusion.96
  151.3 1.0 convolution_reduce_fusion.94
  153.1 1.0 convolution_reduce_fusion.93
  154.9 1.0 convolution_reduce_fusion.92
  156.8 1.0 convolution_reduce_fusion.91
  158.7 1.0 convolution_reduce_fusion.90
  160.5 1.0 convolution_reduce_fusion.89
  162.3 1.0 convolution_reduce_fusion.88
  166.0 1.0 convolution_reduce_fusion.86
  167.9 1.0 convolution_reduce_fusion.85
  169.7 1.0 convolution_reduce_fusion.84
  171.6 1.0 convolution_reduce_fusion.83
  173.4 1.0 convolution_reduce_fusion.82
  175.6 1.0 convolution_reduce_fusion.81
  177.5 1.0 convolution_reduce_fusion.80
  181.2 1.0 convolution_reduce_fusion.78
  183.0 1.0 convolution_reduce_fusion.77
  184.9 1.0 convolution_reduce_fusion.76
  196.0 1.0 convolution_reduce_fusion.70
  209.9 1.0 fusion.2
  210.9 280.1 %psum.59 = f32[64,64]{1,0:T(8,128)S(1)} all-reduce(f32[64,64]{1,0:T(8,128)S(1)} %fusion.289), channel_id=1, replica_groups=mesh['rows'=64,'mass'=8] {'rows'}, use_global_device_ids=true, to_apply=%region_3.0 | all-reduce | flops 4096 | bytes 32768 | tf_op jit(solution)/shard_map/psum | solution.py:32
  494.2 247.9 %all-reduce.7.cloned.1.call-done = f32[64,512]{1,0:T(8,128)} async-done(((f32[64,512]{1,0:T(8,128)}), f32[64,512]{1,0:T(8,128)}) %all-reduce.7.cloned.1.call-update) | async-done | bytes 131088 | tf_op jit(solution)/shard_map/psum | solution.py:32
  754.1 1.3 fusion.270
  844.9 1.3 fusion.4
  846.2 19.4 %psum.61 = f32[64,64]{1,0:T(8,128)S(1)} all-reduce(f32[64,64]{1,0:T(8,128)S(1)} %fusion.290), channel_id=1, replica_groups=mesh['rows'=64,'mass'=8] {'mass'}, use_global_device_ids=true, to_apply=%region_5.0 | all-reduce | flops 4096 | bytes 32768 | tf_op jit(solution)/shard_map/psum | solution.py:25
  868.9 68.7 %all-reduce.9.cloned.1.call-done = f32[64,1536]{1,0:T(8,128)} async-done(((f32[64,1536]{1,0:T(8,128)}), f32[64,1536]{1,0:T(8,128)}) %all-reduce.9.cloned.1.call-update) | async-done | bytes 393232 | tf_op jit(solution)/shard_map/psum | solution.py:25
  937.6 1.3 slice_reduce_fusion.114
  939.9 1.1 convolution_reduce_fusion.62
  977.4 1.0 convolution_reduce_fusion.42
  1007.7 1.0 convolution_reduce_fusion.26
  1011.4 1.0 convolution_reduce_fusion.24
  1020.6 1.0 convolution_reduce_fusion.19
  1032.1 1.0 convolution_reduce_fusion.13
  1054.4 1.0 convolution_reduce_fusion.1
  1058.6 1.0 fusion
  1059.6 280.1 %psum.63 = f32[64,64]{1,0:T(8,128)S(1)} all-reduce(f32[64,64]{1,0:T(8,128)S(1)} %fusion.291), channel_id=1, replica_groups=mesh['rows'=64,'mass'=8] {'rows'}, use_global_device_ids=true, to_apply=%region_7.0 | all-reduce | flops 4096 | bytes 32768 | tf_op jit(solution)/shard_map/psum | solution.py:32
  1342.8 248.0 %all-reduce.11.cloned.1.call-done = f32[64,512]{1,0:T(8,128)} async-done(((f32[64,512]{1,0:T(8,128)}), f32[64,512]{1,0:T(8,128)}) %all-reduce.11.cloned.1.call-update) | async-done | bytes 131088 | tf_op jit(solution)/shard_map/psum | solution.py:32
  1602.9 1.3 fusion.266
  (1168 shorter events, 402.2 us)
Async XLA Ops:
  7.2 2.1 copy-start
  7.2 81.5 %all-reduce.5.cloned.1.call-start = ((), (), s32[]{:S(2)}) async-start(), calls=%async_computation | async-start | bytes 786432 | tf_op jit(solution)/shard_map/psum | solution.py:25
  10.6 731.5 %all-reduce.7.cloned.1.call-start = ((), (), s32[]{:S(2)}) async-start(), calls=%async_computation.1 | async-start | bytes 262144 | tf_op jit(solution)/shard_map/psum | solution.py:32
  35.6 55.3 %copy-start.4 = (f32[64,64]{1,0:T(8,128)}, f32[64,64]{1,0:T(8,128)S(1)}, u32[]{:S(2)}) copy-start(f32[64,64]{1,0:T(8,128)S(1)} %psum.57) | copy-start | bytes 49156
  90.9 12.2 copy-start.7
  491.0 252.8 %copy-start.6 = (f32[64,64]{1,0:T(8,128)}, f32[64,64]{1,0:T(8,128)S(1)}, u32[]{:S(2)}) copy-start(f32[64,64]{1,0:T(8,128)S(1)} %psum.59) | copy-start | bytes 49156
  492.7 444.9 %all-reduce.9.cloned.1.call-start = ((), (), s32[]{:S(2)}) async-start(), calls=%async_computation.2 | async-start | bytes 786432 | tf_op jit(solution)/shard_map/psum | solution.py:25
  756.1 29.3 %copy-start.10 = (f32[64,512]{1,0:T(8,128)S(1)}, f32[64,512]{1,0:T(8,128)}, u32[]{:S(2)}) copy-start(f32[64,512]{1,0:T(8,128)} %all-reduce.7.cloned.1.call-done) | copy-start | bytes 393220
  865.6 74.3 %copy-start.3 = (f32[64,64]{1,0:T(8,128)}, f32[64,64]{1,0:T(8,128)S(1)}, u32[]{:S(2)}) copy-start(f32[64,64]{1,0:T(8,128)S(1)} %psum.61) | copy-start | bytes 49156
  867.8 722.9 %all-reduce.11.cloned.1.call-start = ((), (), s32[]{:S(2)}) async-start(), calls=%async_computation.3 | async-start | bytes 262144 | tf_op jit(solution)/shard_map/psum | solution.py:32
  939.9 12.2 copy-start.8
  1058.1 283.2 %copy-start.1 = (f32[64,1536]{1,0:T(8,128)}, f32[64,1536]{1,0:T(8,128)S(1)}, u32[]{:S(2)}) copy-start(f32[64,1536]{1,0:T(8,128)S(1)} %scatter.1171) | copy-start | bytes 1179652
  1339.7 253.0 %copy-start.5 = (f32[64,64]{1,0:T(8,128)}, f32[64,64]{1,0:T(8,128)S(1)}, u32[]{:S(2)}) copy-start(f32[64,64]{1,0:T(8,128)S(1)} %psum.63) | copy-start | bytes 49156
  1604.8 29.2 %copy-start.9 = (f32[64,512]{1,0:T(8,128)S(1)}, f32[64,512]{1,0:T(8,128)}, u32[]{:S(2)}) copy-start(f32[64,512]{1,0:T(8,128)} %all-reduce.11.cloned.1.call-done) | copy-start | bytes 393220
  1692.8 0.7 copy-start.2
Sparse Core Ops, SparseCore 0:
  10.9 77.7 all-reduce.4
  492.8 249.2 all-reduce.6
  867.9 69.6 all-reduce.8
  1341.5 249.1 all-reduce.10
where the time goes:
time: 1720 us; the launch traced here: 1700 us
  waiting for transfers between devices  615 us (36%)
  blocking collectives  604 us (35%)
  matrix products  242 us (14%)
  other arithmetic  161 us (9%)
  local copies, waits for them, and re-layouts  56.8 us (3%)
  between operations  21.1 us (1%)
    psum x2, blocking collectives, body(): spec_cross, conc_gram = lax.psum((spec_cross, conc_gram), 'rows')  560 us
    psum x2, waiting for transfers between devices, body(): spec_cross, conc_gram = lax.psum((spec_cross, conc_gram), 'rows')  496 us
    dot_general x256, matrix products, sweep_rows(): mixed = jnp.dot(gram[index], factor, precision=lax.Precision.HIGHEST)  236 us
    max x256, other arithmetic, sweep_rows(): factor = factor.at[index].set(jnp.maximum(updated, 0.0001))  161 us
    psum x2, waiting for transfers between devices, body(): conc_cross, spec_gram = lax.psum((conc_cross, spec_gram), 'mass')  119 us
    psum x2, blocking collectives, body(): conc_cross, spec_gram = lax.psum((conc_cross, spec_gram), 'mass')  44.1 us
  transfers between devices with their start and end apart: 4, of which 4 were waited for; matrix products, arithmetic and copies ran while one was open for 0% of the time, Pallas kernels for 0%

commit v1 on v0

v1 whole, which is shorter than its diff:
```python
import jax
import jax.numpy as jnp
from jax import lax
from jax.experimental import pallas as pl
from jax.experimental.pallas import tpu as pltpu
from jax.sharding import PartitionSpec as P

ITERS = 2
COMPS = 64
FLOOR = 1e-4
NT = (((1,), (1,)), ((), ()))
CHUNK = 512

def holder(x, pair, low):
    return x * 16 + pair * 2 + (low ^ (pair >= 4))


NEAR = [[holder(x, pair, low) for x in range(4) for low in range(2)] for pair in range(8)]
FAR = [[holder(x, pair, low) for pair in range(8)] for x in range(4) for low in range(2)]


def gram_of(factor):
    return lax.dot_general(
        factor, factor, NT, precision=lax.Precision.HIGHEST, preferred_element_type=jnp.float32
    )


def sweep(sums, width, old, new, held):
    gram = sums[:, width : width + COMPS]
    rows = lax.broadcasted_iota(jnp.int32, (COMPS, COMPS), 0)
    cols = lax.broadcasted_iota(jnp.int32, (COMPS, COMPS), 1)
    diag = jnp.sum(jnp.where(rows == cols, gram, 0.0), axis=1, keepdims=True)
    inverse = 1.0 / diag
    scaled = gram * inverse
    upper = jnp.where(cols > rows, scaled, 0.0)
    lower = jnp.where(cols < rows, scaled, 0.0)
    held[...] = sums[:, :width] * inverse - jnp.dot(
        upper, old[...], precision=lax.Precision.HIGHEST, preferred_element_type=jnp.float32
    )
    for block in range(0, COMPS, 8):
        own = held[block : block + 8, :]
        for index in range(7):
            row = jnp.maximum(own[index : index + 1, :], FLOOR)
            own = own - lower[block : block + 8, block + index : block + index + 1] * row
        own = jnp.maximum(own, FLOOR)
        new[block : block + 8, :] = own
        for start in range(0, width, CHUNK):
            part = [own[i : i + 1, start : start + CHUNK] for i in range(8)]
            for later in range(block + 8, COMPS, 8):
                total = held[later : later + 8, start : start + CHUNK]
                for i in range(8):
                    total = total - lower[later : later + 8, block + i : block + i + 1] * part[i]
                held[later : later + 8, start : start + CHUNK] = total


def put_spec_terms(spectra, data, out):
    pixels = data.shape[0]
    out[:, :pixels] = lax.dot_general(
        spectra.astype(jnp.bfloat16), data[...], NT, preferred_element_type=jnp.float32
    )
    out[:, pixels : pixels + COMPS] = gram_of(spectra)
    out[:, pixels + COMPS :] = jnp.zeros_like(out[:, pixels + COMPS :])


def put_conc_terms(conc, data, out):
    channels = data.shape[1]
    out[:, :channels] = jnp.dot(
        conc.astype(jnp.bfloat16), data[...], preferred_element_type=jnp.float32
    )
    out[:, channels : channels + COMPS] = gram_of(conc)
    out[:, channels + COMPS :] = jnp.zeros_like(out[:, channels + COMPS :])


def first_kernel(data, spec, out):
    put_spec_terms(spec[...], data, out)


def conc_kernel(sums, old, data, new, out, held):
    sweep(sums, old.shape[1], old, new, held)
    put_conc_terms(new[...], data, out)


def spec_kernel(sums, old, data, new, out, held):
    sweep(sums, old.shape[1], old, new, held)
    put_spec_terms(new[...], data, out)


def last_kernel(sums, old, new, held):
    sweep(sums, old.shape[1], old, new, held)


def f32(*shape):
    return jax.ShapeDtypeStruct(shape, jnp.float32)


def call(kernel, outs, *args, held=None):
    return pl.pallas_call(
        kernel,
        out_shape=outs,
        scratch_shapes=[] if held is None else [pltpu.VMEM(held, jnp.float32)],
        compiler_params=pltpu.CompilerParams(vmem_limit_bytes=24 << 20),
    )(*args)


def padded(width):
    return -(-(width + COMPS) // 128) * 128


def exchange(parts, axis, groups=None):
    return lax.all_to_all(parts, axis, 0, 0, axis_index_groups=groups)


def to_all(share, axis, groups=None):
    return exchange(jnp.broadcast_to(share, (8,) + share.shape), axis, groups)


def sum_mass(terms):
    parts = exchange(terms.reshape(8, 8, -1), "mass")
    return to_all(jnp.sum(parts, axis=0), "mass").reshape(terms.shape)


def sum_rows(terms):
    parts = exchange(terms.reshape(8, 8, -1), "rows", NEAR)
    parts = to_all(jnp.sum(parts, axis=0), "rows", FAR)
    return to_all(jnp.sum(parts, axis=0), "rows", NEAR).reshape(terms.shape)


def body(data, conc, spec):
    pixels, channels = data.shape
    wide, narrow = f32(COMPS, padded(pixels)), f32(COMPS, padded(channels))
    terms = call(first_kernel, wide, data, spec)
    for step in range(ITERS):
        sums = sum_mass(terms)
        conc, terms = call(
            conc_kernel, (f32(*conc.shape), narrow), sums, conc, data, held=conc.shape
        )
        sums = sum_rows(terms)
        if step < ITERS - 1:
            spec, terms = call(
                spec_kernel, (f32(*spec.shape), wide), sums, spec, data, held=spec.shape
            )
        else:
            spec = call(last_kernel, f32(*spec.shape), sums, spec, held=spec.shape)
    return conc, spec


def solution(mesh):
    return jax.shard_map(
        body,
        mesh=mesh,
        in_specs=(P("rows", "mass"), P(None, "rows"), P(None, "mass")),
        out_specs=(P(None, "rows"), P(None, "mass")),
        check_vma=False,
    )
```

time: 1720 us -> 147 us (0.09); the launches traced: 1700 us -> 146 us
  waiting for transfers between devices: 615 us -> 0 us
  blocking collectives: 604 us -> 134 us
  matrix products: 242 us -> 0 us
  other arithmetic: 161 us -> 0.11 us
  local copies, waits for them, and re-layouts: 56.8 us -> 2.43 us
  between operations: 21.1 us -> 0.75 us
    psum x4 -> x0, waiting for transfers between devices: 615 us -> none  [the longest x2 496 us: body(): spec_cross, conc_gram = lax.psum((spec_cross, conc_gram), 'rows')]
    psum x4 -> x0, blocking collectives: 604 us -> none  [the longest x2 560 us: body(): spec_cross, conc_gram = lax.psum((spec_cross, conc_gram), 'rows')]
    dot_general x264 -> x0, matrix products: 242 us -> none  [the longest x256 236 us: sweep_rows(): mixed = jnp.dot(gram[index], factor, precision=lax.Precision.HIGHEST)]
    max x256 -> x0, other arithmetic: 161 us -> none  [sweep_rows(): factor = factor.at[index].set(jnp.maximum(updated, 0.0001))]
    all_to_all x0 -> x10, blocking collectives: none -> 134 us  [exchange(): return lax.all_to_all(parts, axis, 0, 0, axis_index_groups=groups)]
    scatter x256 -> x0, local copies, waits for them, and re-layouts: 29.2 us -> none  [sweep_rows(): factor = factor.at[index].set(jnp.maximum(updated, 0.0001))]
    slice x288 -> x0, local copies, waits for them, and re-layouts: 24 us -> none  [sweep_rows(): updated = factor[index] + (cross[index] - mixed) / gram[index, index]]
  transfers between devices with their start and end apart: 4 -> 0, of which waited for: 4 -> 0; matrix products, arithmetic and copies ran while one was open for 0% -> 0% of each run, Pallas kernels for 0% -> 0%
where the time goes in v1:
time: 147 us; the launch traced here: 146 us
  blocking collectives  134 us (91%)
  Pallas kernels  8.66 us (6%)
  local copies, waits for them, and re-layouts  2.43 us (2%)
    all_to_all x10, blocking collectives, exchange(): return lax.all_to_all(parts, axis, 0, 0, axis_index_groups=groups)  134 us
    pallas_call x5, Pallas kernels, call(): pl.pallas_call(kernel, out_shape=outs, scratch_shapes=[] if held is None...  8.66 us

profile of v1, /device:TPU:24, one launch (start us, length us, event | category | flops | bytes accessed | tf_op | source)
XLA Modules:
  0.0 145.8 jit_solution(4829697240257809780)
XLA Ops:
  0.6 0.0 copy-start
  0.6 1.4 copy-done
  2.0 0.0 copy-start.2
  2.0 0.9 copy-done.2
  2.9 0.7 shard_map.50
  3.6 0.0 copy-start.1
  3.7 0.0 copy-start.4
  3.7 15.3 %all_to_all.50 = f32[8,8,1664]{2,1,0:T(8,128)S(1)} all-to-all(f32[8,8,1664]{2,1,0:T(8,128)S(1)} %bitcast.10), channel_id=1, replica_groups=mesh['rows'=64,'mass'=8] {'mass'}, dimensions={0} | all-to-all | bytes 851968 | tf_op jit(solution)/shard_map/all_to_all | solution.py:110
  19.1 11.7 %all_to_all.51 = f32[8,8,1664]{2,1,0:T(8,128)S(1)} all-to-all(f32[8,8,1664]{2,1,0:T(8,128)S(1)} %broadcast_in_dim.18), channel_id=1, replica_groups=mesh['rows'=64,'mass'=8] {'mass'}, dimensions={0} | all-to-all | bytes 851968 | tf_op jit(solution)/shard_map/all_to_all | solution.py:110
  30.8 0.0 copy-done.1
  30.8 0.0 copy-done.4
  30.8 0.0 copy-start.3
  30.8 2.5 %shard_map.51 = (f32[64,1536]{1,0:T(8,128)S(1)}, f32[64,640]{1,0:T(8,128)S(1)}) custom-call(f32[64,1664]{1,0:T(8,128)S(1)} %bitcast.9, f32[64,1536]{1,0:T(8,128)S(1)} %copy-done.4, bf16[1536,512]{1,0:T(8,128)(2,1)S(1)} %copy-done.1), custom_call_target="tpu_custom_call" | custom-call | tf_op jit(solution)/shard_map/pallas_call | solution.py:97
  33.3 9.2 %all_to_all.52 = f32[8,8,640]{2,1,0:T(8,128)S(1)} all-to-all(f32[8,8,640]{2,1,0:T(8,128)S(1)} %bitcast.15), channel_id=1, replica_groups={{0,8,128,136,256,264,384,392},{16,24,144,152,272,280,400,408},{32,40,16..., dimensions={0} | all-to-all | bytes 327680 | tf_op jit(solution)/shard_map/all_to_all | solution.py:110
  42.5 28.2 %all_to_all.53 = f32[8,8,640]{2,1,0:T(8,128)S(1)} all-to-all(f32[8,8,640]{2,1,0:T(8,128)S(1)} %broadcast_in_dim.19), channel_id=1, replica_groups={{0,16,32,48,72,88,104,120},{8,24,40,56,64,80,96,112},{128,144,160,176,2..., dimensions={0} | all-to-all | bytes 327680 | tf_op jit(solution)/shard_map/all_to_all | solution.py:110
  70.8 9.5 %all_to_all.54 = f32[8,8,640]{2,1,0:T(8,128)S(1)} all-to-all(f32[8,8,640]{2,1,0:T(8,128)S(1)} %broadcast_in_dim.20), channel_id=1, replica_groups={{0,8,128,136,256,264,384,392},{16,24,144,152,272,280,400,408},{32,40,16..., dimensions={0} | all-to-all | bytes 327680 | tf_op jit(solution)/shard_map/all_to_all | solution.py:110
  80.3 0.0 copy-done.3
  80.3 1.4 shard_map.52
  81.6 11.7 %all_to_all.55 = f32[8,8,1664]{2,1,0:T(8,128)S(1)} all-to-all(f32[8,8,1664]{2,1,0:T(8,128)S(1)} %bitcast.13), channel_id=1, replica_groups=mesh['rows'=64,'mass'=8] {'mass'}, dimensions={0} | all-to-all | bytes 851968 | tf_op jit(solution)/shard_map/all_to_all | solution.py:110
  93.4 11.7 %all_to_all.56 = f32[8,8,1664]{2,1,0:T(8,128)S(1)} all-to-all(f32[8,8,1664]{2,1,0:T(8,128)S(1)} %broadcast_in_dim.21), channel_id=1, replica_groups=mesh['rows'=64,'mass'=8] {'mass'}, dimensions={0} | all-to-all | bytes 851968 | tf_op jit(solution)/shard_map/all_to_all | solution.py:110
  105.1 2.6 %shard_map.53 = (f32[64,1536]{1,0:T(8,128)}, f32[64,640]{1,0:T(8,128)S(1)}) custom-call(f32[64,1664]{1,0:T(8,128)S(1)} %bitcast.8, f32[64,1536]{1,0:T(8,128)S(1)} %get-tuple-element.10.old, bf16[1536,512]{1,0:T(8,128)(2,1)S(1)} %copy-done.1), custom_call_target="tpu_custom_call" | custom-call | tf_op jit(solution)/shard_map/pallas_call | solution.py:97
  107.7 9.3 %all_to_all.57 = f32[8,8,640]{2,1,0:T(8,128)S(1)} all-to-all(f32[8,8,640]{2,1,0:T(8,128)S(1)} %bitcast.14), channel_id=1, replica_groups={{0,8,128,136,256,264,384,392},{16,24,144,152,272,280,400,408},{32,40,16..., dimensions={0} | all-to-all | bytes 327680 | tf_op jit(solution)/shard_map/all_to_all | solution.py:110
  117.1 17.1 %all_to_all.58 = f32[8,8,640]{2,1,0:T(8,128)S(1)} all-to-all(f32[8,8,640]{2,1,0:T(8,128)S(1)} %broadcast_in_dim.22), channel_id=1, replica_groups={{0,16,32,48,72,88,104,120},{8,24,40,56,64,80,96,112},{128,144,160,176,2..., dimensions={0} | all-to-all | bytes 327680 | tf_op jit(solution)/shard_map/all_to_all | solution.py:110
  134.2 10.2 %all_to_all.59 = f32[8,8,640]{2,1,0:T(8,128)S(1)} all-to-all(f32[8,8,640]{2,1,0:T(8,128)S(1)} %broadcast_in_dim.23), channel_id=1, replica_groups={{0,8,128,136,256,264,384,392},{16,24,144,152,272,280,400,408},{32,40,16..., dimensions={0} | all-to-all | bytes 327680 | tf_op jit(solution)/shard_map/all_to_all | solution.py:110
  144.4 1.5 %shard_map.54 = f32[64,512]{1,0:T(8,128)} custom-call(f32[64,640]{1,0:T(8,128)S(1)} %bitcast.12, f32[64,512]{1,0:T(8,128)S(1)} %get-tuple-element.13.old), custom_call_target="tpu_custom_call" | custom-call | tf_op jit(solution)/shard_map/pallas_call | solution.py:97
  (12 shorter events, 0.2 us)
Async XLA Ops:
  0.6 1.4 copy-start
  2.0 0.9 copy-start.2
  3.6 27.1 %copy-start.1 = (bf16[1536,512]{1,0:T(8,128)(2,1)S(1)}, bf16[1536,512]{1,0:T(8,128)(2,1)}, u32[]{:S(2)}) copy-start(bf16[1536,512]{1,0:T(8,128)(2,1)} %data.7) | copy-start | bytes 4718596
  3.7 27.1 %copy-start.4 = (f32[64,1536]{1,0:T(8,128)S(1)}, f32[64,1536]{1,0:T(8,128)}, u32[]{:S(2)}) copy-start(f32[64,1536]{1,0:T(8,128)} %old.2) | copy-start | bytes 1179652
  30.8 49.5 %copy-start.3 = (f32[64,512]{1,0:T(8,128)S(1)}, f32[64,512]{1,0:T(8,128)}, u32[]{:S(2)}) copy-start(f32[64,512]{1,0:T(8,128)} %old.3) | copy-start | bytes 393220

commit v2 on v1

v2 whole, which is shorter than its diff:
```python
import jax
import jax.numpy as jnp
from jax import lax
from jax.experimental import pallas as pl
from jax.experimental.pallas import tpu as pltpu
from jax.sharding import PartitionSpec as P

ITERS = 2
COMPS = 64
FLOOR = 1e-4
NT = (((1,), (1,)), ((), ()))
LANES = 128
CHUNK = 256


def holder(x, pair, low):
    return x * 16 + pair * 2 + (low ^ (pair >= 4))


NEAR = [[holder(x, pair, low) for x in range(4) for low in range(2)] for pair in range(8)]
FAR = [[holder(x, pair, low) for pair in range(8)] for x in range(4) for low in range(2)]
COLUMN = [[y * 2 + core for y in range(4)] for core in range(2)]
SIBLING = [(i, i ^ 1) for i in range(8)]


def gram_of(factor):
    return lax.dot_general(
        factor, factor, NT, precision=lax.Precision.HIGHEST, preferred_element_type=jnp.float32
    )


def half_rows(index, half):
    return pl.ds(pl.multiple_of(index * half, half), half)


def tiles_of(width):
    return COMPS // 8 * (width // LANES) + COMPS // 16


def put_cross_tiles(out, cross):
    across = cross.shape[1] // LANES
    for i in range(COMPS // 8):
        for j in range(across):
            out[i * across + j] = cross[i * 8 : i * 8 + 8, j * LANES : (j + 1) * LANES]


def put_gram_tiles(out, gram, first):
    for i in range(COMPS // 16):
        out[first + i] = jnp.concatenate(
            [gram[i * 16 : i * 16 + 8, :], gram[i * 16 + 8 : i * 16 + 16, :]], axis=1
        )


def take_tiles(tile, width):
    across = width // LANES
    cross = jnp.concatenate(
        [
            jnp.concatenate([tile(i * across + j) for j in range(across)], axis=1)
            for i in range(COMPS // 8)
        ],
        axis=0,
    )
    first = COMPS // 8 * across
    gram = []
    for i in range(COMPS // 16):
        pair = tile(first + i)
        gram += [pair[:, :COMPS], pair[:, COMPS:]]
    return cross, jnp.concatenate(gram, axis=0)


def pieces_of(width):
    return 2 * (width // LANES) + 1


def put_pieces(out, cross, gram):
    across = cross.shape[1] // LANES
    for share in range(8):
        for low in range(2):
            rows = slice(share * 8 + low * 4, share * 8 + low * 4 + 4)
            for j in range(across):
                out[share, 2 * j + low] = cross[rows, j * LANES : (j + 1) * LANES]
        upper, lower = gram[share * 8 : share * 8 + 4, :], gram[share * 8 + 4 : share * 8 + 8, :]
        out[share, 2 * across] = jnp.concatenate([upper, lower], axis=1)


def take_pieces(pieces, width):
    across = width // LANES
    cross, gram = [], []
    for share in range(8):
        tiles = [
            jnp.concatenate([pieces[share, 2 * j], pieces[share, 2 * j + 1]], axis=0)
            for j in range(across)
        ]
        cross.append(jnp.concatenate(tiles, axis=1))
        both = pieces[share, 2 * across]
        gram += [both[:, :COMPS], both[:, COMPS:]]
    return jnp.concatenate(cross, axis=0), jnp.concatenate(gram, axis=0)


def sweep(cross, gram, old, new, held, done=None):
    width = cross.shape[1]
    rows = lax.broadcasted_iota(jnp.int32, (COMPS, COMPS), 0)
    cols = lax.broadcasted_iota(jnp.int32, (COMPS, COMPS), 1)
    diag = jnp.sum(jnp.where(rows == cols, gram, 0.0), axis=1, keepdims=True)
    inverse = 1.0 / diag
    scaled = gram * inverse
    upper = jnp.where(cols > rows, scaled, 0.0)
    lower = jnp.where(cols < rows, scaled, 0.0)
    held[...] = cross * inverse - jnp.dot(
        upper, old, precision=lax.Precision.HIGHEST, preferred_element_type=jnp.float32
    )
    for block in range(0, COMPS, 8):
        own = held[block : block + 8, :]
        for index in range(7):
            row = jnp.maximum(own[index : index + 1, :], FLOOR)
            own = own - lower[block : block + 8, block + index : block + index + 1] * row
        own = jnp.maximum(own, FLOOR)
        new[block : block + 8, :] = own
        if done is not None:
            done(block // 8)
        for start in range(0, width, CHUNK):
            part = [own[i : i + 1, start : start + CHUNK] for i in range(8)]
            for later in range(block + 8, COMPS, 8):
                total = held[later : later + 8, start : start + CHUNK]
                for i in range(8):
                    total = total - lower[later : later + 8, block + i : block + i + 1] * part[i]
                held[later : later + 8, start : start + CHUNK] = total


def spec_cross(low, data):
    return lax.dot_general(low, data, NT, preferred_element_type=jnp.float32)


def spec_terms(core, spectra, data, out):
    half = data.shape[0] // 2
    cross = spec_cross(spectra.astype(jnp.bfloat16), data[half_rows(core, half), :])
    put_cross_tiles(out, cross)


def first_kernel(core, spec, data, send):
    spec_terms(1 - core[0], spec[...], data, send)
    put_gram_tiles(send, gram_of(spec[...]), send.shape[0] - COMPS // 16)


def spec_kernel(core, sums, old, data, new, send, held):
    cross, gram = take_pieces(sums, old.shape[1])
    sweep(cross, gram, old[...], new, held)
    first_kernel(core, new, data, send)


def keep_kernel(core, spec, data, send, keep):
    spec_terms(core[0], spec[...], data, keep)
    first = keep.shape[0] - COMPS // 16
    keep[first:] = send[first:]


def conc_sweep_kernel(core, parts, old, new, held):
    half = new.shape[1]
    cross, gram = take_tiles(
        lambda i: (parts[0, i] + parts[1, i]) + (parts[2, i] + parts[3, i]), half
    )
    if old.shape[1] == half:
        before = old[...]
    else:
        before = old[:, half_rows(core[0], half)]
    sweep(cross, gram, before, new, held)


def conc_terms(core, part, data):
    half = part.shape[1]
    cross = jnp.dot(
        part.astype(jnp.bfloat16), data[half_rows(core, half), :], preferred_element_type=jnp.float32
    )
    return cross, gram_of(part)


def own_terms_kernel(core, own, data, out):
    channels = data.shape[1]
    cross, gram = conc_terms(core[0], own[...], data)
    out[:, :channels] = cross
    out[:, channels : channels + COMPS] = gram
    out[:, channels + COMPS :] = jnp.zeros_like(out[:, channels + COMPS :])


def all_terms_kernel(core, other, data, own_terms, out):
    channels = data.shape[1]
    cross, gram = conc_terms(1 - core[0], other[...], data)
    put_pieces(
        out,
        own_terms[:, :channels] + cross,
        own_terms[:, channels : channels + COMPS] + gram,
    )


def last_kernel(core, sums, old, own, other, conc, spec, new, held, sems):
    half = own.shape[1]
    copies = [
        pltpu.make_async_copy(part, conc.at[:, half_rows(index, half)], sems.at[i])
        for i, (part, index) in enumerate(((own, core[0]), (other, 1 - core[0])))
    ]
    for copy in copies:
        copy.start()

    def done(block):
        rows = pl.ds(block * 8, 8)
        copies.append(pltpu.make_async_copy(new.at[rows, :], spec.at[rows, :], sems.at[2 + block]))
        copies[-1].start()

    cross, gram = take_pieces(sums, old.shape[1])
    sweep(cross, gram, old[...], new, held, done)
    for copy in copies:
        copy.wait()


def f32(*shape):
    return jax.ShapeDtypeStruct(shape, jnp.float32)


VMEM = pl.BlockSpec(memory_space=pltpu.VMEM)
SMEM = pl.BlockSpec(memory_space=pltpu.SMEM)
HBM = pl.BlockSpec(memory_space=pltpu.HBM)


def call(kernel, outs, specs, scratch, *args, space=VMEM):
    return pl.pallas_call(
        kernel,
        out_shape=outs,
        in_specs=specs,
        out_specs=jax.tree.map(lambda _: space, outs),
        scratch_shapes=scratch,
        compiler_params=pltpu.CompilerParams(vmem_limit_bytes=24 << 20),
        cost_estimate=pl.CostEstimate(
            flops=200_000_000, bytes_accessed=2_000_000, transcendentals=0
        ),
    )(*args)


def exchange(parts, axis, groups):
    return lax.all_to_all(parts, axis, 0, 0, axis_index_groups=groups)


def to_all(share, axis, groups):
    members = len(groups[0])
    return exchange(jnp.broadcast_to(share, (members,) + share.shape), axis, groups)


def swap(half):
    return lax.ppermute(half, "mass", SIBLING)


def sum_rows(terms):
    parts = exchange(terms, "rows", NEAR)
    parts = to_all(jnp.sum(parts, axis=0), "rows", FAR)
    return to_all(jnp.sum(parts, axis=0), "rows", NEAR)


def body(data, conc, spec):
    pixels, channels = data.shape
    half = pixels // 2
    core = lax.rem(lax.axis_index("mass"), 2).reshape(1)
    tiles, narrow = f32(tiles_of(half), 8, LANES), f32(COMPS, channels + LANES)
    pieces = f32(8, pieces_of(channels), 4, LANES)
    held = pltpu.VMEM((COMPS, half), jnp.float32)
    spec_held = pltpu.VMEM(spec.shape, jnp.float32)
    send = call(first_kernel, tiles, [SMEM, VMEM, VMEM], [], core, spec, data)
    own = conc
    for step in range(ITERS):
        arriving = swap(send)
        keep = call(keep_kernel, tiles, [SMEM, VMEM, VMEM, VMEM], [], core, spec, data, send)
        parts = to_all(keep + arriving, "mass", COLUMN)
        own = call(
            conc_sweep_kernel, f32(COMPS, half), [SMEM, VMEM, VMEM], [held], core, parts, own
        )
        other = swap(own)
        terms = call(own_terms_kernel, narrow, [SMEM, VMEM, VMEM], [], core, own, data)
        terms = call(
            all_terms_kernel, pieces, [SMEM, VMEM, VMEM, VMEM], [], core, other, data, terms
        )
        sums = sum_rows(terms)
        if step < ITERS - 1:
            spec, send = call(
                spec_kernel,
                (f32(*spec.shape), tiles),
                [SMEM, VMEM, VMEM, VMEM],
                [spec_held],
                core,
                sums,
                spec,
                data,
            )
        else:
            conc, spec = call(
                last_kernel,
                (f32(*conc.shape), f32(*spec.shape)),
                [SMEM, VMEM, VMEM, VMEM, VMEM],
                [spec_held, spec_held, pltpu.SemaphoreType.DMA((10,))],
                core,
                sums,
                spec,
                own,
                other,
                space=HBM,
            )
    return conc, spec


def solution(mesh):
    return jax.shard_map(
        body,
        mesh=mesh,
        in_specs=(P("rows", "mass"), P(None, "rows"), P(None, "mass")),
        out_specs=(P(None, "rows"), P(None, "mass")),
        check_vma=False,
    )
```

time: 147 us -> 143 us (0.973)
  blocking collectives: 134 us -> 118 us
  starting transfers between devices: 0 us -> 7.73 us
  waiting for transfers between devices: 0 us -> 4.06 us
    all_to_all x10 -> x8, blocking collectives: 134 us -> 118 us  [exchange(): return lax.all_to_all(parts, axis, 0, 0, axis_index_groups=groups)]
    ppermute x0 -> x4, starting transfers between devices: none -> 7.73 us  [swap(): return lax.ppermute(half, 'mass', SIBLING)]
    ppermute x0 -> x4, waiting for transfers between devices: none -> 4.06 us  [swap(): return lax.ppermute(half, 'mass', SIBLING)]
    pallas_call x5 -> x11, Pallas kernels: 8.66 us -> 7.97 us  [call(): pl.pallas_call(kernel, out_shape=outs, in_specs=specs, out_specs=jax.tree...]
  transfers between devices with their start and end apart: 0 -> 4, of which waited for: 0 -> 4; matrix products, arithmetic and copies ran while one was open for 0% -> 0% of each run, Pallas kernels for 0% -> 1%
where the time goes in v2:
time: 143 us; the launch traced here: 142 us
  blocking collectives  118 us (83%)
  Pallas kernels  7.97 us (6%)
  starting transfers between devices  7.73 us (5%)
  waiting for transfers between devices  4.06 us (3%)
  local copies, waits for them, and re-layouts  2.52 us (2%)
    all_to_all x8, blocking collectives, exchange(): return lax.all_to_all(parts, axis, 0, 0, axis_index_groups=groups)  118 us
    pallas_call x11, Pallas kernels, call(): pl.pallas_call(kernel, out_shape=outs, in_specs=specs, out_specs=jax.tree...  7.97 us
    ppermute x4, starting transfers between devices, swap(): return lax.ppermute(half, 'mass', SIBLING)  7.73 us
    ppermute x4, waiting for transfers between devices, swap(): return lax.ppermute(half, 'mass', SIBLING)  4.06 us
  transfers between devices with their start and end apart: 4, of which 4 were waited for; matrix products, arithmetic and copies ran while one was open for 0% of the time, Pallas kernels for 1%

profile of v2, /device:TPU:24, one launch (start us, length us, event | category | flops | bytes accessed | tf_op | source)
XLA Modules:
  0.0 141.7 jit_solution(5622924447978127890)
XLA Ops:
  0.6 0.0 copy-start
  0.6 1.4 copy-done
  2.0 0.0 copy-start.2
  2.0 0.9 copy-done.2
  2.9 0.5 shard_map.50.send
  3.5 1.9 %collective-permute-start = (f32[52,8,128]{2,1,0:T(8,128)S(1)}, f32[52,8,128]{2,1,0:T(8,128)S(1)}, u32[]{:S(2)}, u32[]{:S(2)}) collective-permute-start(f32[52,8,128]{2,1,0:T(8,128)S(1)} %shard_map.50.send), channel_id=1, source_target_pairs={{0,1},{1,0},{2,3},{3,2},{4,5},{5,4},{6,7},{7,6},{8,9},{9,8},{10,11... | collective-permute-start | bytes 638984 | tf_op jit(solution)/shard_map/ppermute | solution.py:248
  5.4 0.3 shard_map.51
  5.8 0.0 copy-start.4
  5.8 1.1 collective-permute-done
  6.9 0.1 broadcast_in_dim.18
  6.9 0.0 copy-start.1
  6.9 19.6 %all_to_all.40.parts = f32[4,52,8,128]{3,2,1,0:T(8,128)S(1)} all-to-all(f32[4,52,8,128]{3,2,1,0:T(8,128)S(1)} %broadcast_in_dim.18), channel_id=1, replica_groups={{0,2,4,6},{1,3,5,7},{8,10,12,14},{9,11,13,15},{16,18,20,22},{17,19,21,2..., dimensions={0} | all-to-all | bytes 1703936 | tf_op jit(solution)/shard_map/all_to_all | solution.py:239
  26.6 0.0 copy-done.4
  26.6 1.0 shard_map.52.own.old
  27.6 1.9 %collective-permute-start.1 = (f32[64,768]{1,0:T(8,128)S(1)}, f32[64,768]{1,0:T(8,128)S(1)}, u32[]{:S(2)}, u32[]{:S(2)}) collective-permute-start(f32[64,768]{1,0:T(8,128)S(1)} %shard_map.52.own.old), channel_id=1, source_target_pairs={{0,1},{1,0},{2,3},{3,2},{4,5},{5,4},{6,7},{7,6},{8,9},{9,8},{10,11... | collective-permute-start | bytes 589832 | tf_op jit(solution)/shard_map/ppermute | solution.py:248
  29.5 0.0 copy-done.1
  29.5 0.4 shard_map.53.own_terms
  30.0 0.0 copy-start.3
  30.0 0.9 collective-permute-done.1.other
  30.9 0.5 shard_map.54
  31.4 9.2 %all_to_all.41 = f32[8,9,4,128]{3,2,1,0:T(4,128)S(1)} all-to-all(f32[8,9,4,128]{3,2,1,0:T(4,128)S(1)} %shard_map.54), channel_id=1, replica_groups={{0,8,128,136,256,264,384,392},{16,24,144,152,272,280,400,408},{32,40,16..., dimensions={0} | all-to-all | bytes 294912 | tf_op jit(solution)/shard_map/all_to_all | solution.py:239
  40.6 27.4 %all_to_all.42 = f32[8,9,4,128]{3,2,1,0:T(4,128)S(1)} all-to-all(f32[8,9,4,128]{3,2,1,0:T(4,128)S(1)} %broadcast_in_dim.19), channel_id=1, replica_groups={{0,16,32,48,72,88,104,120},{8,24,40,56,64,80,96,112},{128,144,160,176,2..., dimensions={0} | all-to-all | bytes 294912 | tf_op jit(solution)/shard_map/all_to_all | solution.py:239
  68.1 9.7 %all_to_all.43.sums = f32[8,9,4,128]{3,2,1,0:T(4,128)S(1)} all-to-all(f32[8,9,4,128]{3,2,1,0:T(4,128)S(1)} %broadcast_in_dim.20), channel_id=1, replica_groups={{0,8,128,136,256,264,384,392},{16,24,144,152,272,280,400,408},{32,40,16..., dimensions={0} | all-to-all | bytes 294912 | tf_op jit(solution)/shard_map/all_to_all | solution.py:239
  77.8 0.0 copy-done.3
  77.8 1.3 shard_map.55
  79.1 2.0 %collective-permute-start.2 = (f32[52,8,128]{2,1,0:T(8,128)S(1)}, f32[52,8,128]{2,1,0:T(8,128)S(1)}, u32[]{:S(2)}, u32[]{:S(2)}) collective-permute-start(f32[52,8,128]{2,1,0:T(8,128)S(1)} %get-tuple-element.5.send), channel_id=1, source_target_pairs={{0,1},{1,0},{2,3},{3,2},{4,5},{5,4},{6,7},{7,6},{8,9},{9,8},{10,11... | collective-permute-start | bytes 638984 | tf_op jit(solution)/shard_map/ppermute | solution.py:248
  81.0 0.3 shard_map.56
  81.4 1.1 collective-permute-done.2
  82.5 0.1 broadcast_in_dim.21
  82.6 16.0 %all_to_all.44.parts = f32[4,52,8,128]{3,2,1,0:T(8,128)S(1)} all-to-all(f32[4,52,8,128]{3,2,1,0:T(8,128)S(1)} %broadcast_in_dim.21), channel_id=1, replica_groups={{0,2,4,6},{1,3,5,7},{8,10,12,14},{9,11,13,15},{16,18,20,22},{17,19,21,2..., dimensions={0} | all-to-all | bytes 1703936 | tf_op jit(solution)/shard_map/all_to_all | solution.py:239
  98.5 1.0 shard_map.57.own
  99.6 1.9 %collective-permute-start.3 = (f32[64,768]{1,0:T(8,128)S(1)}, f32[64,768]{1,0:T(8,128)S(1)}, u32[]{:S(2)}, u32[]{:S(2)}) collective-permute-start(f32[64,768]{1,0:T(8,128)S(1)} %shard_map.57.own), channel_id=1, source_target_pairs={{0,1},{1,0},{2,3},{3,2},{4,5},{5,4},{6,7},{7,6},{8,9},{9,8},{10,11... | collective-permute-start | bytes 589832 | tf_op jit(solution)/shard_map/ppermute | solution.py:248
  101.5 0.4 shard_map.58.own_terms
  101.9 1.0 collective-permute-done.3.other
  102.9 0.5 shard_map.59
  103.4 9.2 %all_to_all.45 = f32[8,9,4,128]{3,2,1,0:T(4,128)S(1)} all-to-all(f32[8,9,4,128]{3,2,1,0:T(4,128)S(1)} %shard_map.59), channel_id=1, replica_groups={{0,8,128,136,256,264,384,392},{16,24,144,152,272,280,400,408},{32,40,16..., dimensions={0} | all-to-all | bytes 294912 | tf_op jit(solution)/shard_map/all_to_all | solution.py:239
  112.7 17.6 %all_to_all.46 = f32[8,9,4,128]{3,2,1,0:T(4,128)S(1)} all-to-all(f32[8,9,4,128]{3,2,1,0:T(4,128)S(1)} %broadcast_in_dim.22), channel_id=1, replica_groups={{0,16,32,48,72,88,104,120},{8,24,40,56,64,80,96,112},{128,144,160,176,2..., dimensions={0} | all-to-all | bytes 294912 | tf_op jit(solution)/shard_map/all_to_all | solution.py:239
  130.4 9.7 %all_to_all.47.sums = f32[8,9,4,128]{3,2,1,0:T(4,128)S(1)} all-to-all(f32[8,9,4,128]{3,2,1,0:T(4,128)S(1)} %broadcast_in_dim.23), channel_id=1, replica_groups={{0,8,128,136,256,264,384,392},{16,24,144,152,272,280,400,408},{32,40,16..., dimensions={0} | all-to-all | bytes 294912 | tf_op jit(solution)/shard_map/all_to_all | solution.py:239
  140.1 1.6 %shard_map.60 = (f32[64,1536]{1,0:T(8,128)}, f32[64,512]{1,0:T(8,128)}) custom-call(s32[1]{0:T(128)} %bitcast.core, f32[8,9,4,128]{3,2,1,0:T(4,128)S(1)} %all_to_all.47.sums, f32[64,512]{1,0:T(8,128)S(1)} %get-tuple-element.4.spec.old, f32[64,768]{1,0:T(8,128)S(1)} %shard_map.57.own, f32[64,768]{1,0:T(8,128)S(1)} %collective-permute-done.3.other), custom_call_target="tpu_custom_call" | custom-call | flops 200000000 | bytes 2000000 | tf_op jit(solution)/shard_map/pallas_call | solution.py:225
  (10 shorter events, 0.3 us)
Async XLA Ops:
  0.6 1.4 copy-start
  2.0 0.9 copy-start.2
  3.5 3.4 %collective-permute-start = (f32[52,8,128]{2,1,0:T(8,128)S(1)}, f32[52,8,128]{2,1,0:T(8,128)S(1)}, u32[]{:S(2)}, u32[]{:S(2)}) collective-permute-start(f32[52,8,128]{2,1,0:T(8,128)S(1)} %shard_map.50.send), channel_id=1, source_target_pairs={{0,1},{1,0},{2,3},{3,2},{4,5},{5,4},{6,7},{7,6},{8,9},{9,8},{10,11... | collective-permute-start | bytes 638984 | tf_op jit(solution)/shard_map/ppermute | solution.py:248
  5.8 20.8 %copy-start.4 = (f32[64,1536]{1,0:T(8,128)S(1)}, f32[64,1536]{1,0:T(8,128)}, u32[]{:S(2)}) copy-start(f32[64,1536]{1,0:T(8,128)} %old.2) | copy-start | bytes 1179652
  6.9 22.6 %copy-start.1 = (bf16[1536,512]{1,0:T(8,128)(2,1)S(1)}, bf16[1536,512]{1,0:T(8,128)(2,1)}, u32[]{:S(2)}) copy-start(bf16[1536,512]{1,0:T(8,128)(2,1)} %data.15) | copy-start | bytes 4718596
  27.6 3.3 %collective-permute-start.1 = (f32[64,768]{1,0:T(8,128)S(1)}, f32[64,768]{1,0:T(8,128)S(1)}, u32[]{:S(2)}, u32[]{:S(2)}) collective-permute-start(f32[64,768]{1,0:T(8,128)S(1)} %shard_map.52.own.old), channel_id=1, source_target_pairs={{0,1},{1,0},{2,3},{3,2},{4,5},{5,4},{6,7},{7,6},{8,9},{9,8},{10,11... | collective-permute-start | bytes 589832 | tf_op jit(solution)/shard_map/ppermute | solution.py:248
  30.0 47.8 %copy-start.3 = (f32[64,512]{1,0:T(8,128)S(1)}, f32[64,512]{1,0:T(8,128)}, u32[]{:S(2)}) copy-start(f32[64,512]{1,0:T(8,128)} %old.3) | copy-start | bytes 393220
  79.1 3.4 %collective-permute-start.2 = (f32[52,8,128]{2,1,0:T(8,128)S(1)}, f32[52,8,128]{2,1,0:T(8,128)S(1)}, u32[]{:S(2)}, u32[]{:S(2)}) collective-permute-start(f32[52,8,128]{2,1,0:T(8,128)S(1)} %get-tuple-element.5.send), channel_id=1, source_target_pairs={{0,1},{1,0},{2,3},{3,2},{4,5},{5,4},{6,7},{7,6},{8,9},{9,8},{10,11... | collective-permute-start | bytes 638984 | tf_op jit(solution)/shard_map/ppermute | solution.py:248
  99.6 3.3 %collective-permute-start.3 = (f32[64,768]{1,0:T(8,128)S(1)}, f32[64,768]{1,0:T(8,128)S(1)}, u32[]{:S(2)}, u32[]{:S(2)}) collective-permute-start(f32[64,768]{1,0:T(8,128)S(1)} %shard_map.57.own), channel_id=1, source_target_pairs={{0,1},{1,0},{2,3},{3,2},{4,5},{5,4},{6,7},{7,6},{8,9},{9,8},{10,11... | collective-permute-start | bytes 589832 | tf_op jit(solution)/shard_map/ppermute | solution.py:248

commit v3 on v2

--- a/solution.py
+++ b/solution.py
@@ -17,9 +17,11 @@
     return x * 16 + pair * 2 + (low ^ (pair >= 4))
 
 
-NEAR = [[holder(x, pair, low) for x in range(4) for low in range(2)] for pair in range(8)]
-FAR = [[holder(x, pair, low) for pair in range(8)] for x in range(4) for low in range(2)]
-COLUMN = [[y * 2 + core for y in range(4)] for core in range(2)]
+MIDDLE = (2, 3, 0, 1)
+MIDDLE_PAIRS = (4, 5, 6, 7, 0, 1, 2, 3)
+NEAR = [[holder(x, pair, low) for x in MIDDLE for low in range(2)] for pair in range(8)]
+FAR = [[holder(x, pair, low) for pair in MIDDLE_PAIRS] for x in range(4) for low in range(2)]
+COLUMN = [[y * 2 + core for y in MIDDLE] for core in range(2)]
 SIBLING = [(i, i ^ 1) for i in range(8)]
 
 

time: 143 us -> 135 us (0.944)
  blocking collectives: 118 us -> 110 us
    all_to_all x8, blocking collectives: 118 us -> 110 us  [exchange(): return lax.all_to_all(parts, axis, 0, 0, axis_index_groups=groups)]
where the time goes in v3:
time: 135 us; the launch traced here: 134 us
  blocking collectives  110 us (81%)
  Pallas kernels  7.97 us (6%)
  starting transfers between devices  7.73 us (6%)
  waiting for transfers between devices  4.06 us (3%)
  local copies, waits for them, and re-layouts  2.52 us (2%)
    all_to_all x8, blocking collectives, exchange(): return lax.all_to_all(parts, axis, 0, 0, axis_index_groups=groups)  110 us
    pallas_call x11, Pallas kernels, call(): pl.pallas_call(kernel, out_shape=outs, in_specs=specs, out_specs=jax.tree...  7.97 us
    ppermute x4, starting transfers between devices, swap(): return lax.ppermute(half, 'mass', SIBLING)  7.73 us
    ppermute x4, waiting for transfers between devices, swap(): return lax.ppermute(half, 'mass', SIBLING)  4.06 us
  transfers between devices with their start and end apart: 4, of which 4 were waited for; matrix products, arithmetic and copies ran while one was open for 0% of the time, Pallas kernels for 1%

profile of v3, /device:TPU:24, one launch (start us, length us, event | category | flops | bytes accessed | tf_op | source)
XLA Modules:
  0.0 133.8 jit_solution(8193903632904946892)
XLA Ops:
  0.6 0.0 copy-start
  0.6 1.4 %copy-done = bf16[1536,512]{1,0:T(8,128)(2,1)S(1)} copy-done((bf16[1536,512]{1,0:T(8,128)(2,1)S(1)}, bf16[1536,512]{1,0:T(8,128)(2,1)}, u32[]{:S(2)}) %copy-start) | copy-done | bytes 1572888
  2.0 0.0 copy-start.2
  2.0 0.9 copy-done.2
  2.9 0.5 shard_map.50.send
  3.5 1.9 %collective-permute-start = (f32[52,8,128]{2,1,0:T(8,128)S(1)}, f32[52,8,128]{2,1,0:T(8,128)S(1)}, u32[]{:S(2)}, u32[]{:S(2)}) collective-permute-start(f32[52,8,128]{2,1,0:T(8,128)S(1)} %shard_map.50.send), channel_id=1, source_target_pairs={{0,1},{1,0},{2,3},{3,2},{4,5},{5,4},{6,7},{7,6},{8,9},{9,8},{10,11... | collective-permute-start | bytes 638984 | tf_op jit(solution)/shard_map/ppermute | solution.py:250
  5.4 0.3 shard_map.51
  5.8 0.0 copy-start.4
  5.8 1.1 collective-permute-done
  6.9 0.1 broadcast_in_dim.18
  6.9 0.0 copy-start.1
  6.9 19.8 %all_to_all.40.parts = f32[4,52,8,128]{3,2,1,0:T(8,128)S(1)} all-to-all(f32[4,52,8,128]{3,2,1,0:T(8,128)S(1)} %broadcast_in_dim.18), channel_id=1, replica_groups={{4,6,0,2},{5,7,1,3},{12,14,8,10},{13,15,9,11},{20,22,16,18},{21,23,17,1..., dimensions={0} | all-to-all | bytes 1703936 | tf_op jit(solution)/shard_map/all_to_all | solution.py:241
  26.8 0.0 copy-done.4
  26.8 1.0 shard_map.52.own.old
  27.8 1.9 %collective-permute-start.1 = (f32[64,768]{1,0:T(8,128)S(1)}, f32[64,768]{1,0:T(8,128)S(1)}, u32[]{:S(2)}, u32[]{:S(2)}) collective-permute-start(f32[64,768]{1,0:T(8,128)S(1)} %shard_map.52.own.old), channel_id=1, source_target_pairs={{0,1},{1,0},{2,3},{3,2},{4,5},{5,4},{6,7},{7,6},{8,9},{9,8},{10,11... | collective-permute-start | bytes 589832 | tf_op jit(solution)/shard_map/ppermute | solution.py:250
  29.7 0.0 copy-done.1
  29.7 0.4 shard_map.53.own_terms
  30.2 0.0 copy-start.3
  30.2 1.0 collective-permute-done.1.other
  31.1 0.5 shard_map.54
  31.6 8.6 %all_to_all.41 = f32[8,9,4,128]{3,2,1,0:T(4,128)S(1)} all-to-all(f32[8,9,4,128]{3,2,1,0:T(4,128)S(1)} %shard_map.54), channel_id=1, replica_groups={{256,264,384,392,0,8,128,136},{272,280,400,408,16,24,144,152},{288,296,..., dimensions={0} | all-to-all | bytes 294912 | tf_op jit(solution)/shard_map/all_to_all | solution.py:241
  40.3 20.7 %all_to_all.42 = f32[8,9,4,128]{3,2,1,0:T(4,128)S(1)} all-to-all(f32[8,9,4,128]{3,2,1,0:T(4,128)S(1)} %broadcast_in_dim.19), channel_id=1, replica_groups={{72,88,104,120,0,16,32,48},{64,80,96,112,8,24,40,56},{200,216,232,248,1..., dimensions={0} | all-to-all | bytes 294912 | tf_op jit(solution)/shard_map/all_to_all | solution.py:241
  61.0 9.3 %all_to_all.43.sums = f32[8,9,4,128]{3,2,1,0:T(4,128)S(1)} all-to-all(f32[8,9,4,128]{3,2,1,0:T(4,128)S(1)} %broadcast_in_dim.20), channel_id=1, replica_groups={{256,264,384,392,0,8,128,136},{272,280,400,408,16,24,144,152},{288,296,..., dimensions={0} | all-to-all | bytes 294912 | tf_op jit(solution)/shard_map/all_to_all | solution.py:241
  70.3 0.0 copy-done.3
  70.3 1.3 shard_map.55
  71.6 2.0 %collective-permute-start.2 = (f32[52,8,128]{2,1,0:T(8,128)S(1)}, f32[52,8,128]{2,1,0:T(8,128)S(1)}, u32[]{:S(2)}, u32[]{:S(2)}) collective-permute-start(f32[52,8,128]{2,1,0:T(8,128)S(1)} %get-tuple-element.5.send), channel_id=1, source_target_pairs={{0,1},{1,0},{2,3},{3,2},{4,5},{5,4},{6,7},{7,6},{8,9},{9,8},{10,11... | collective-permute-start | bytes 638984 | tf_op jit(solution)/shard_map/ppermute | solution.py:250
  73.6 0.3 shard_map.56
  73.9 1.1 collective-permute-done.2
  75.0 0.1 broadcast_in_dim.21
  75.1 16.0 %all_to_all.44.parts = f32[4,52,8,128]{3,2,1,0:T(8,128)S(1)} all-to-all(f32[4,52,8,128]{3,2,1,0:T(8,128)S(1)} %broadcast_in_dim.21), channel_id=1, replica_groups={{4,6,0,2},{5,7,1,3},{12,14,8,10},{13,15,9,11},{20,22,16,18},{21,23,17,1..., dimensions={0} | all-to-all | bytes 1703936 | tf_op jit(solution)/shard_map/all_to_all | solution.py:241
  91.1 1.0 shard_map.57.own
  92.1 1.9 %collective-permute-start.3 = (f32[64,768]{1,0:T(8,128)S(1)}, f32[64,768]{1,0:T(8,128)S(1)}, u32[]{:S(2)}, u32[]{:S(2)}) collective-permute-start(f32[64,768]{1,0:T(8,128)S(1)} %shard_map.57.own), channel_id=1, source_target_pairs={{0,1},{1,0},{2,3},{3,2},{4,5},{5,4},{6,7},{7,6},{8,9},{9,8},{10,11... | collective-permute-start | bytes 589832 | tf_op jit(solution)/shard_map/ppermute | solution.py:250
  94.0 0.4 shard_map.58.own_terms
  94.4 1.0 collective-permute-done.3.other
  95.4 0.5 shard_map.59
  95.9 9.0 %all_to_all.45 = f32[8,9,4,128]{3,2,1,0:T(4,128)S(1)} all-to-all(f32[8,9,4,128]{3,2,1,0:T(4,128)S(1)} %shard_map.59), channel_id=1, replica_groups={{256,264,384,392,0,8,128,136},{272,280,400,408,16,24,144,152},{288,296,..., dimensions={0} | all-to-all | bytes 294912 | tf_op jit(solution)/shard_map/all_to_all | solution.py:241
  105.0 18.1 %all_to_all.46 = f32[8,9,4,128]{3,2,1,0:T(4,128)S(1)} all-to-all(f32[8,9,4,128]{3,2,1,0:T(4,128)S(1)} %broadcast_in_dim.22), channel_id=1, replica_groups={{72,88,104,120,0,16,32,48},{64,80,96,112,8,24,40,56},{200,216,232,248,1..., dimensions={0} | all-to-all | bytes 294912 | tf_op jit(solution)/shard_map/all_to_all | solution.py:241
  123.1 9.0 %all_to_all.47.sums = f32[8,9,4,128]{3,2,1,0:T(4,128)S(1)} all-to-all(f32[8,9,4,128]{3,2,1,0:T(4,128)S(1)} %broadcast_in_dim.23), channel_id=1, replica_groups={{256,264,384,392,0,8,128,136},{272,280,400,408,16,24,144,152},{288,296,..., dimensions={0} | all-to-all | bytes 294912 | tf_op jit(solution)/shard_map/all_to_all | solution.py:241
  132.2 1.6 %shard_map.60 = (f32[64,1536]{1,0:T(8,128)}, f32[64,512]{1,0:T(8,128)}) custom-call(s32[1]{0:T(128)} %bitcast.core, f32[8,9,4,128]{3,2,1,0:T(4,128)S(1)} %all_to_all.47.sums, f32[64,512]{1,0:T(8,128)S(1)} %get-tuple-element.4.spec.old, f32[64,768]{1,0:T(8,128)S(1)} %shard_map.57.own, f32[64,768]{1,0:T(8,128)S(1)} %collective-permute-done.3.other), custom_call_target="tpu_custom_call" | custom-call | flops 200000000 | bytes 2000000 | tf_op jit(solution)/shard_map/pallas_call | solution.py:227
  (10 shorter events, 0.3 us)
Async XLA Ops:
  0.6 1.4 %copy-start = (bf16[1536,512]{1,0:T(8,128)(2,1)S(1)}, bf16[1536,512]{1,0:T(8,128)(2,1)}, u32[]{:S(2)}) copy-start(bf16[1536,512]{1,0:T(8,128)(2,1)} %data.15) | copy-start | bytes 4718596
  2.0 0.9 copy-start.2
  3.5 3.4 %collective-permute-start = (f32[52,8,128]{2,1,0:T(8,128)S(1)}, f32[52,8,128]{2,1,0:T(8,128)S(1)}, u32[]{:S(2)}, u32[]{:S(2)}) collective-permute-start(f32[52,8,128]{2,1,0:T(8,128)S(1)} %shard_map.50.send), channel_id=1, source_target_pairs={{0,1},{1,0},{2,3},{3,2},{4,5},{5,4},{6,7},{7,6},{8,9},{9,8},{10,11... | collective-permute-start | bytes 638984 | tf_op jit(solution)/shard_map/ppermute | solution.py:250
  5.8 21.0 %copy-start.4 = (f32[64,1536]{1,0:T(8,128)S(1)}, f32[64,1536]{1,0:T(8,128)}, u32[]{:S(2)}) copy-start(f32[64,1536]{1,0:T(8,128)} %old.2) | copy-start | bytes 1179652
  6.9 22.8 %copy-start.1 = (bf16[1536,512]{1,0:T(8,128)(2,1)S(1)}, bf16[1536,512]{1,0:T(8,128)(2,1)}, u32[]{:S(2)}) copy-start(bf16[1536,512]{1,0:T(8,128)(2,1)} %data.15) | copy-start | bytes 4718596
  27.8 3.3 %collective-permute-start.1 = (f32[64,768]{1,0:T(8,128)S(1)}, f32[64,768]{1,0:T(8,128)S(1)}, u32[]{:S(2)}, u32[]{:S(2)}) collective-permute-start(f32[64,768]{1,0:T(8,128)S(1)} %shard_map.52.own.old), channel_id=1, source_target_pairs={{0,1},{1,0},{2,3},{3,2},{4,5},{5,4},{6,7},{7,6},{8,9},{9,8},{10,11... | collective-permute-start | bytes 589832 | tf_op jit(solution)/shard_map/ppermute | solution.py:250
  30.2 40.1 %copy-start.3 = (f32[64,512]{1,0:T(8,128)S(1)}, f32[64,512]{1,0:T(8,128)}, u32[]{:S(2)}) copy-start(f32[64,512]{1,0:T(8,128)} %old.3) | copy-start | bytes 393220
  71.6 3.4 %collective-permute-start.2 = (f32[52,8,128]{2,1,0:T(8,128)S(1)}, f32[52,8,128]{2,1,0:T(8,128)S(1)}, u32[]{:S(2)}, u32[]{:S(2)}) collective-permute-start(f32[52,8,128]{2,1,0:T(8,128)S(1)} %get-tuple-element.5.send), channel_id=1, source_target_pairs={{0,1},{1,0},{2,3},{3,2},{4,5},{5,4},{6,7},{7,6},{8,9},{9,8},{10,11... | collective-permute-start | bytes 638984 | tf_op jit(solution)/shard_map/ppermute | solution.py:250
  92.1 3.3 %collective-permute-start.3 = (f32[64,768]{1,0:T(8,128)S(1)}, f32[64,768]{1,0:T(8,128)S(1)}, u32[]{:S(2)}, u32[]{:S(2)}) collective-permute-start(f32[64,768]{1,0:T(8,128)S(1)} %shard_map.57.own), channel_id=1, source_target_pairs={{0,1},{1,0},{2,3},{3,2},{4,5},{5,4},{6,7},{7,6},{8,9},{9,8},{10,11... | collective-permute-start | bytes 589832 | tf_op jit(solution)/shard_map/ppermute | solution.py:250

commit v4 on v2

--- a/solution.py
+++ b/solution.py
@@ -17,9 +17,11 @@
     return x * 16 + pair * 2 + (low ^ (pair >= 4))
 
 
-NEAR = [[holder(x, pair, low) for x in range(4) for low in range(2)] for pair in range(8)]
-FAR = [[holder(x, pair, low) for pair in range(8)] for x in range(4) for low in range(2)]
-COLUMN = [[y * 2 + core for y in range(4)] for core in range(2)]
+FROM_MIDDLE = (2, 0, 1, 3)
+PAIRS_FROM_MIDDLE = (4, 0, 5, 1, 6, 2, 7, 3)
+NEAR = [[holder(x, pair, low) for low in range(2) for x in FROM_MIDDLE] for pair in range(8)]
+FAR = [[holder(x, pair, low) for pair in PAIRS_FROM_MIDDLE] for x in range(4) for low in range(2)]
+COLUMN = [[y * 2 + core for y in FROM_MIDDLE] for core in range(2)]
 SIBLING = [(i, i ^ 1) for i in range(8)]
 
 

time: 143 us -> 134 us (0.937)
  blocking collectives: 118 us -> 110 us
    all_to_all x8, blocking collectives: 118 us -> 110 us  [exchange(): return lax.all_to_all(parts, axis, 0, 0, axis_index_groups=groups)]
where the time goes in v4:
time: 134 us; the launch traced here: 133 us
  blocking collectives  110 us (82%)
  Pallas kernels  7.96 us (6%)
  starting transfers between devices  7.73 us (6%)
  waiting for transfers between devices  4.06 us (3%)
  local copies, waits for them, and re-layouts  2.52 us (2%)
    all_to_all x8, blocking collectives, exchange(): return lax.all_to_all(parts, axis, 0, 0, axis_index_groups=groups)  110 us
    pallas_call x11, Pallas kernels, call(): pl.pallas_call(kernel, out_shape=outs, in_specs=specs, out_specs=jax.tree...  7.96 us
    ppermute x4, starting transfers between devices, swap(): return lax.ppermute(half, 'mass', SIBLING)  7.73 us
    ppermute x4, waiting for transfers between devices, swap(): return lax.ppermute(half, 'mass', SIBLING)  4.06 us
  transfers between devices with their start and end apart: 4, of which 4 were waited for; matrix products, arithmetic and copies ran while one was open for 0% of the time, Pallas kernels for 1%

profile of v4, /device:TPU:24, one launch (start us, length us, event | category | flops | bytes accessed | tf_op | source)
XLA Modules:
  0.0 132.8 jit_solution(10802244054248926207)
XLA Ops:
  0.6 0.0 copy-start
  0.6 1.4 %copy-done = bf16[1536,512]{1,0:T(8,128)(2,1)S(1)} copy-done((bf16[1536,512]{1,0:T(8,128)(2,1)S(1)}, bf16[1536,512]{1,0:T(8,128)(2,1)}, u32[]{:S(2)}) %copy-start) | copy-done | bytes 1572888
  2.0 0.0 copy-start.2
  2.0 0.9 copy-done.2
  2.9 0.5 shard_map.50.send
  3.5 1.9 %collective-permute-start = (f32[52,8,128]{2,1,0:T(8,128)S(1)}, f32[52,8,128]{2,1,0:T(8,128)S(1)}, u32[]{:S(2)}, u32[]{:S(2)}) collective-permute-start(f32[52,8,128]{2,1,0:T(8,128)S(1)} %shard_map.50.send), channel_id=1, source_target_pairs={{0,1},{1,0},{2,3},{3,2},{4,5},{5,4},{6,7},{7,6},{8,9},{9,8},{10,11... | collective-permute-start | bytes 638984 | tf_op jit(solution)/shard_map/ppermute | solution.py:250
  5.4 0.3 shard_map.51
  5.8 0.0 copy-start.4
  5.8 1.1 collective-permute-done
  6.9 0.1 broadcast_in_dim.18
  6.9 0.0 copy-start.1
  6.9 19.7 %all_to_all.40.parts = f32[4,52,8,128]{3,2,1,0:T(8,128)S(1)} all-to-all(f32[4,52,8,128]{3,2,1,0:T(8,128)S(1)} %broadcast_in_dim.18), channel_id=1, replica_groups={{4,0,2,6},{5,1,3,7},{12,8,10,14},{13,9,11,15},{20,16,18,22},{21,17,19,2..., dimensions={0} | all-to-all | bytes 1703936 | tf_op jit(solution)/shard_map/all_to_all | solution.py:241
  26.7 0.0 copy-done.4
  26.7 1.0 shard_map.52.own.old
  27.7 1.9 %collective-permute-start.1 = (f32[64,768]{1,0:T(8,128)S(1)}, f32[64,768]{1,0:T(8,128)S(1)}, u32[]{:S(2)}, u32[]{:S(2)}) collective-permute-start(f32[64,768]{1,0:T(8,128)S(1)} %shard_map.52.own.old), channel_id=1, source_target_pairs={{0,1},{1,0},{2,3},{3,2},{4,5},{5,4},{6,7},{7,6},{8,9},{9,8},{10,11... | collective-permute-start | bytes 589832 | tf_op jit(solution)/shard_map/ppermute | solution.py:250
  29.6 0.0 copy-done.1
  29.6 0.4 shard_map.53.own_terms
  30.1 0.0 copy-start.3
  30.1 0.9 collective-permute-done.1.other
  31.0 0.5 shard_map.54
  31.6 8.6 %all_to_all.41 = f32[8,9,4,128]{3,2,1,0:T(4,128)S(1)} all-to-all(f32[8,9,4,128]{3,2,1,0:T(4,128)S(1)} %shard_map.54), channel_id=1, replica_groups={{256,0,128,384,264,8,136,392},{272,16,144,400,280,24,152,408},{288,32,1..., dimensions={0} | all-to-all | bytes 294912 | tf_op jit(solution)/shard_map/all_to_all | solution.py:241
  40.2 20.9 %all_to_all.42 = f32[8,9,4,128]{3,2,1,0:T(4,128)S(1)} all-to-all(f32[8,9,4,128]{3,2,1,0:T(4,128)S(1)} %broadcast_in_dim.19), channel_id=1, replica_groups={{72,0,88,16,104,32,120,48},{64,8,80,24,96,40,112,56},{200,128,216,144,2..., dimensions={0} | all-to-all | bytes 294912 | tf_op jit(solution)/shard_map/all_to_all | solution.py:241
  61.2 9.1 %all_to_all.43.sums = f32[8,9,4,128]{3,2,1,0:T(4,128)S(1)} all-to-all(f32[8,9,4,128]{3,2,1,0:T(4,128)S(1)} %broadcast_in_dim.20), channel_id=1, replica_groups={{256,0,128,384,264,8,136,392},{272,16,144,400,280,24,152,408},{288,32,1..., dimensions={0} | all-to-all | bytes 294912 | tf_op jit(solution)/shard_map/all_to_all | solution.py:241
  70.3 0.0 copy-done.3
  70.3 1.3 shard_map.55
  71.6 2.0 %collective-permute-start.2 = (f32[52,8,128]{2,1,0:T(8,128)S(1)}, f32[52,8,128]{2,1,0:T(8,128)S(1)}, u32[]{:S(2)}, u32[]{:S(2)}) collective-permute-start(f32[52,8,128]{2,1,0:T(8,128)S(1)} %get-tuple-element.5.send), channel_id=1, source_target_pairs={{0,1},{1,0},{2,3},{3,2},{4,5},{5,4},{6,7},{7,6},{8,9},{9,8},{10,11... | collective-permute-start | bytes 638984 | tf_op jit(solution)/shard_map/ppermute | solution.py:250
  73.6 0.3 shard_map.56
  73.9 1.1 collective-permute-done.2
  75.0 0.1 broadcast_in_dim.21
  75.1 16.0 %all_to_all.44.parts = f32[4,52,8,128]{3,2,1,0:T(8,128)S(1)} all-to-all(f32[4,52,8,128]{3,2,1,0:T(8,128)S(1)} %broadcast_in_dim.21), channel_id=1, replica_groups={{4,0,2,6},{5,1,3,7},{12,8,10,14},{13,9,11,15},{20,16,18,22},{21,17,19,2..., dimensions={0} | all-to-all | bytes 1703936 | tf_op jit(solution)/shard_map/all_to_all | solution.py:241
  91.1 1.0 shard_map.57.own
  92.1 1.9 %collective-permute-start.3 = (f32[64,768]{1,0:T(8,128)S(1)}, f32[64,768]{1,0:T(8,128)S(1)}, u32[]{:S(2)}, u32[]{:S(2)}) collective-permute-start(f32[64,768]{1,0:T(8,128)S(1)} %shard_map.57.own), channel_id=1, source_target_pairs={{0,1},{1,0},{2,3},{3,2},{4,5},{5,4},{6,7},{7,6},{8,9},{9,8},{10,11... | collective-permute-start | bytes 589832 | tf_op jit(solution)/shard_map/ppermute | solution.py:250
  94.0 0.4 shard_map.58.own_terms
  94.4 1.0 collective-permute-done.3.other
  95.4 0.5 shard_map.59
  95.9 9.0 %all_to_all.45 = f32[8,9,4,128]{3,2,1,0:T(4,128)S(1)} all-to-all(f32[8,9,4,128]{3,2,1,0:T(4,128)S(1)} %shard_map.59), channel_id=1, replica_groups={{256,0,128,384,264,8,136,392},{272,16,144,400,280,24,152,408},{288,32,1..., dimensions={0} | all-to-all | bytes 294912 | tf_op jit(solution)/shard_map/all_to_all | solution.py:241
  105.0 17.3 %all_to_all.46 = f32[8,9,4,128]{3,2,1,0:T(4,128)S(1)} all-to-all(f32[8,9,4,128]{3,2,1,0:T(4,128)S(1)} %broadcast_in_dim.22), channel_id=1, replica_groups={{72,0,88,16,104,32,120,48},{64,8,80,24,96,40,112,56},{200,128,216,144,2..., dimensions={0} | all-to-all | bytes 294912 | tf_op jit(solution)/shard_map/all_to_all | solution.py:241
  122.3 8.9 %all_to_all.47.sums = f32[8,9,4,128]{3,2,1,0:T(4,128)S(1)} all-to-all(f32[8,9,4,128]{3,2,1,0:T(4,128)S(1)} %broadcast_in_dim.23), channel_id=1, replica_groups={{256,0,128,384,264,8,136,392},{272,16,144,400,280,24,152,408},{288,32,1..., dimensions={0} | all-to-all | bytes 294912 | tf_op jit(solution)/shard_map/all_to_all | solution.py:241
  131.3 1.6 %shard_map.60 = (f32[64,1536]{1,0:T(8,128)}, f32[64,512]{1,0:T(8,128)}) custom-call(s32[1]{0:T(128)} %bitcast.core, f32[8,9,4,128]{3,2,1,0:T(4,128)S(1)} %all_to_all.47.sums, f32[64,512]{1,0:T(8,128)S(1)} %get-tuple-element.4.spec.old, f32[64,768]{1,0:T(8,128)S(1)} %shard_map.57.own, f32[64,768]{1,0:T(8,128)S(1)} %collective-permute-done.3.other), custom_call_target="tpu_custom_call" | custom-call | flops 200000000 | bytes 2000000 | tf_op jit(solution)/shard_map/pallas_call | solution.py:227
  (10 shorter events, 0.3 us)
Async XLA Ops:
  0.6 1.4 %copy-start = (bf16[1536,512]{1,0:T(8,128)(2,1)S(1)}, bf16[1536,512]{1,0:T(8,128)(2,1)}, u32[]{:S(2)}) copy-start(bf16[1536,512]{1,0:T(8,128)(2,1)} %data.15) | copy-start | bytes 4718596
  2.0 0.9 copy-start.2
  3.5 3.4 %collective-permute-start = (f32[52,8,128]{2,1,0:T(8,128)S(1)}, f32[52,8,128]{2,1,0:T(8,128)S(1)}, u32[]{:S(2)}, u32[]{:S(2)}) collective-permute-start(f32[52,8,128]{2,1,0:T(8,128)S(1)} %shard_map.50.send), channel_id=1, source_target_pairs={{0,1},{1,0},{2,3},{3,2},{4,5},{5,4},{6,7},{7,6},{8,9},{9,8},{10,11... | collective-permute-start | bytes 638984 | tf_op jit(solution)/shard_map/ppermute | solution.py:250
  5.8 20.9 %copy-start.4 = (f32[64,1536]{1,0:T(8,128)S(1)}, f32[64,1536]{1,0:T(8,128)}, u32[]{:S(2)}) copy-start(f32[64,1536]{1,0:T(8,128)} %old.2) | copy-start | bytes 1179652
  6.9 22.7 %copy-start.1 = (bf16[1536,512]{1,0:T(8,128)(2,1)S(1)}, bf16[1536,512]{1,0:T(8,128)(2,1)}, u32[]{:S(2)}) copy-start(bf16[1536,512]{1,0:T(8,128)(2,1)} %data.15) | copy-start | bytes 4718596
  27.7 3.3 %collective-permute-start.1 = (f32[64,768]{1,0:T(8,128)S(1)}, f32[64,768]{1,0:T(8,128)S(1)}, u32[]{:S(2)}, u32[]{:S(2)}) collective-permute-start(f32[64,768]{1,0:T(8,128)S(1)} %shard_map.52.own.old), channel_id=1, source_target_pairs={{0,1},{1,0},{2,3},{3,2},{4,5},{5,4},{6,7},{7,6},{8,9},{9,8},{10,11... | collective-permute-start | bytes 589832 | tf_op jit(solution)/shard_map/ppermute | solution.py:250
  30.1 40.2 %copy-start.3 = (f32[64,512]{1,0:T(8,128)S(1)}, f32[64,512]{1,0:T(8,128)}, u32[]{:S(2)}) copy-start(f32[64,512]{1,0:T(8,128)} %old.3) | copy-start | bytes 393220
  71.6 3.4 %collective-permute-start.2 = (f32[52,8,128]{2,1,0:T(8,128)S(1)}, f32[52,8,128]{2,1,0:T(8,128)S(1)}, u32[]{:S(2)}, u32[]{:S(2)}) collective-permute-start(f32[52,8,128]{2,1,0:T(8,128)S(1)} %get-tuple-element.5.send), channel_id=1, source_target_pairs={{0,1},{1,0},{2,3},{3,2},{4,5},{5,4},{6,7},{7,6},{8,9},{9,8},{10,11... | collective-permute-start | bytes 638984 | tf_op jit(solution)/shard_map/ppermute | solution.py:250
  92.1 3.3 %collective-permute-start.3 = (f32[64,768]{1,0:T(8,128)S(1)}, f32[64,768]{1,0:T(8,128)S(1)}, u32[]{:S(2)}, u32[]{:S(2)}) collective-permute-start(f32[64,768]{1,0:T(8,128)S(1)} %shard_map.57.own), channel_id=1, source_target_pairs={{0,1},{1,0},{2,3},{3,2},{4,5},{5,4},{6,7},{7,6},{8,9},{9,8},{10,11... | collective-permute-start | bytes 589832 | tf_op jit(solution)/shard_map/ppermute | solution.py:250

commit v5 on v4

--- a/solution.py
+++ b/solution.py
@@ -21,7 +21,7 @@
 PAIRS_FROM_MIDDLE = (4, 0, 5, 1, 6, 2, 7, 3)
 NEAR = [[holder(x, pair, low) for low in range(2) for x in FROM_MIDDLE] for pair in range(8)]
 FAR = [[holder(x, pair, low) for pair in PAIRS_FROM_MIDDLE] for x in range(4) for low in range(2)]
-COLUMN = [[y * 2 + core for y in FROM_MIDDLE] for core in range(2)]
+COLUMN = [[y * 2 for y in FROM_MIDDLE], [y * 2 + 1 for y in (2, 0, 3, 1)]]
 SIBLING = [(i, i ^ 1) for i in range(8)]
 
 
@@ -133,25 +133,31 @@
     return lax.dot_general(low, data, NT, preferred_element_type=jnp.float32)
 
 
-def spec_terms(core, spectra, data, out):
+def spec_terms(core, low, data, out):
     half = data.shape[0] // 2
-    cross = spec_cross(spectra.astype(jnp.bfloat16), data[half_rows(core, half), :])
-    put_cross_tiles(out, cross)
-
-
-def first_kernel(core, spec, data, send):
-    spec_terms(1 - core[0], spec[...], data, send)
-    put_gram_tiles(send, gram_of(spec[...]), send.shape[0] - COMPS // 16)
+    put_cross_tiles(out, spec_cross(low, data[half_rows(core, half), :]))
+
+
+def gram_kernel(spec, gram, low):
+    put_gram_tiles(gram, gram_of(spec[...]), 0)
+    low[...] = spec[...].astype(jnp.bfloat16)
+
+
+def first_kernel(core, low, gram, data, send):
+    spec_terms(1 - core[0], low[...], data, send)
+    send[send.shape[0] - COMPS // 16 :] = gram[...]
 
 
 def spec_kernel(core, sums, old, data, new, send, held):
     cross, gram = take_pieces(sums, old.shape[1])
     sweep(cross, gram, old[...], new, held)
-    first_kernel(core, new, data, send)
+    spectra = new[...]
+    spec_terms(1 - core[0], spectra.astype(jnp.bfloat16), data, send)
+    put_gram_tiles(send, gram_of(spectra), send.shape[0] - COMPS // 16)
 
 
 def keep_kernel(core, spec, data, send, keep):
-    spec_terms(core[0], spec[...], data, keep)
+    spec_terms(core[0], spec[...].astype(jnp.bfloat16), data, keep)
     first = keep.shape[0] - COMPS // 16
     keep[first:] = send[first:]
 
@@ -223,7 +229,7 @@
 HBM = pl.BlockSpec(memory_space=pltpu.HBM)
 
 
-def call(kernel, outs, specs, scratch, *args, space=VMEM):
+def call(kernel, outs, specs, scratch, *args, space=VMEM, flops=200_000_000):
     return pl.pallas_call(
         kernel,
         out_shape=outs,
@@ -232,7 +238,7 @@
         scratch_shapes=scratch,
         compiler_params=pltpu.CompilerParams(vmem_limit_bytes=24 << 20),
         cost_estimate=pl.CostEstimate(
-            flops=200_000_000, bytes_accessed=2_000_000, transcendentals=0
+            flops=flops, bytes_accessed=2_000_000, transcendentals=0
         ),
     )(*args)
 
@@ -264,7 +270,15 @@
     pieces = f32(8, pieces_of(channels), 4, LANES)
     held = pltpu.VMEM((COMPS, half), jnp.float32)
     spec_held = pltpu.VMEM(spec.shape, jnp.float32)
-    send = call(first_kernel, tiles, [SMEM, VMEM, VMEM], [], core, spec, data)
+    gram, low = call(
+        gram_kernel,
+        (f32(COMPS // 16, 8, LANES), jax.ShapeDtypeStruct(spec.shape, jnp.bfloat16)),
+        [VMEM],
+        [],
+        spec,
+        flops=4_000_000_000,
+    )
+    send = call(first_kernel, tiles, [SMEM, VMEM, VMEM, VMEM], [], core, low, gram, data)
     own = conc
     for step in range(ITERS):
         arriving = swap(send)

time: 134 us -> 134 us (level)
    pallas_call x11 -> x12, Pallas kernels: 7.96 us -> 8.11 us  [call(): pl.pallas_call(kernel, out_shape=outs, in_specs=specs, out_specs=jax.tree...]
where the time goes in v5:
time: 134 us; the launch traced here: 133 us
  blocking collectives  109 us (81%)
  Pallas kernels  8.11 us (6%)
  starting transfers between devices  7.73 us (6%)
  waiting for transfers between devices  4.07 us (3%)
  local copies, waits for them, and re-layouts  2.18 us (2%)
    all_to_all x8, blocking collectives, exchange(): return lax.all_to_all(parts, axis, 0, 0, axis_index_groups=groups)  109 us
    pallas_call x12, Pallas kernels, call(): pl.pallas_call(kernel, out_shape=outs, in_specs=specs, out_specs=jax.tree...  8.11 us
    ppermute x4, starting transfers between devices, swap(): return lax.ppermute(half, 'mass', SIBLING)  7.73 us
    ppermute x4, waiting for transfers between devices, swap(): return lax.ppermute(half, 'mass', SIBLING)  4.07 us
  transfers between devices with their start and end apart: 4, of which 4 were waited for; matrix products, arithmetic and copies ran while one was open for 0% of the time, Pallas kernels for 1%

profile of v5, /device:TPU:24, one launch (start us, length us, event | category | flops | bytes accessed | tf_op | source)
XLA Modules:
  0.0 132.5 jit_solution(7364518367715044682)
XLA Ops:
  0.6 0.0 copy-start.1
  0.6 0.9 copy-done.1
  1.5 0.0 copy-start
  1.5 0.3 shard_map.50
  1.9 0.0 copy-start.2
  1.9 1.1 copy-done
  2.9 0.3 shard_map.51.send
  3.3 1.9 %collective-permute-start = (f32[52,8,128]{2,1,0:T(8,128)S(1)}, f32[52,8,128]{2,1,0:T(8,128)S(1)}, u32[]{:S(2)}, u32[]{:S(2)}) collective-permute-start(f32[52,8,128]{2,1,0:T(8,128)S(1)} %shard_map.51.send), channel_id=1, source_target_pairs={{0,1},{1,0},{2,3},{3,2},{4,5},{5,4},{6,7},{7,6},{8,9},{9,8},{10,11... | collective-permute-start | bytes 638984 | tf_op jit(solution)/shard_map/ppermute | solution.py:256
  5.2 0.0 copy-done.2
  5.2 0.3 shard_map.52
  5.6 0.0 copy-start.3
  5.6 1.1 collective-permute-done
  6.7 0.1 broadcast_in_dim.18
  6.8 19.6 %all_to_all.40.parts = f32[4,52,8,128]{3,2,1,0:T(8,128)S(1)} all-to-all(f32[4,52,8,128]{3,2,1,0:T(8,128)S(1)} %broadcast_in_dim.18), channel_id=1, replica_groups={{4,0,2,6},{5,1,7,3},{12,8,10,14},{13,9,15,11},{20,16,18,22},{21,17,23,1..., dimensions={0} | all-to-all | bytes 1703936 | tf_op jit(solution)/shard_map/all_to_all | solution.py:247
  26.4 0.0 copy-done.3
  26.4 1.0 shard_map.53.own.old
  27.4 1.9 %collective-permute-start.1 = (f32[64,768]{1,0:T(8,128)S(1)}, f32[64,768]{1,0:T(8,128)S(1)}, u32[]{:S(2)}, u32[]{:S(2)}) collective-permute-start(f32[64,768]{1,0:T(8,128)S(1)} %shard_map.53.own.old), channel_id=1, source_target_pairs={{0,1},{1,0},{2,3},{3,2},{4,5},{5,4},{6,7},{7,6},{8,9},{9,8},{10,11... | collective-permute-start | bytes 589832 | tf_op jit(solution)/shard_map/ppermute | solution.py:256
  29.3 0.4 shard_map.54.own_terms
  29.7 1.0 collective-permute-done.1.other
  30.7 0.5 shard_map.55
  31.2 8.6 %all_to_all.41 = f32[8,9,4,128]{3,2,1,0:T(4,128)S(1)} all-to-all(f32[8,9,4,128]{3,2,1,0:T(4,128)S(1)} %shard_map.55), channel_id=1, replica_groups={{256,0,128,384,264,8,136,392},{272,16,144,400,280,24,152,408},{288,32,1..., dimensions={0} | all-to-all | bytes 294912 | tf_op jit(solution)/shard_map/all_to_all | solution.py:247
  39.9 20.9 %all_to_all.42 = f32[8,9,4,128]{3,2,1,0:T(4,128)S(1)} all-to-all(f32[8,9,4,128]{3,2,1,0:T(4,128)S(1)} %broadcast_in_dim.19), channel_id=1, replica_groups={{72,0,88,16,104,32,120,48},{64,8,80,24,96,40,112,56},{200,128,216,144,2..., dimensions={0} | all-to-all | bytes 294912 | tf_op jit(solution)/shard_map/all_to_all | solution.py:247
  60.9 9.1 %all_to_all.43.sums = f32[8,9,4,128]{3,2,1,0:T(4,128)S(1)} all-to-all(f32[8,9,4,128]{3,2,1,0:T(4,128)S(1)} %broadcast_in_dim.20), channel_id=1, replica_groups={{256,0,128,384,264,8,136,392},{272,16,144,400,280,24,152,408},{288,32,1..., dimensions={0} | all-to-all | bytes 294912 | tf_op jit(solution)/shard_map/all_to_all | solution.py:247
  70.0 1.3 shard_map.56
  71.3 2.0 %collective-permute-start.2 = (f32[52,8,128]{2,1,0:T(8,128)S(1)}, f32[52,8,128]{2,1,0:T(8,128)S(1)}, u32[]{:S(2)}, u32[]{:S(2)}) collective-permute-start(f32[52,8,128]{2,1,0:T(8,128)S(1)} %get-tuple-element.9.send), channel_id=1, source_target_pairs={{0,1},{1,0},{2,3},{3,2},{4,5},{5,4},{6,7},{7,6},{8,9},{9,8},{10,11... | collective-permute-start | bytes 638984 | tf_op jit(solution)/shard_map/ppermute | solution.py:256
  73.3 0.4 shard_map.57
  73.6 1.1 collective-permute-done.2
  74.7 0.1 broadcast_in_dim.21
  74.8 16.0 %all_to_all.44.parts = f32[4,52,8,128]{3,2,1,0:T(8,128)S(1)} all-to-all(f32[4,52,8,128]{3,2,1,0:T(8,128)S(1)} %broadcast_in_dim.21), channel_id=1, replica_groups={{4,0,2,6},{5,1,7,3},{12,8,10,14},{13,9,15,11},{20,16,18,22},{21,17,23,1..., dimensions={0} | all-to-all | bytes 1703936 | tf_op jit(solution)/shard_map/all_to_all | solution.py:247
  90.7 1.0 shard_map.58.own
  91.8 1.9 %collective-permute-start.3 = (f32[64,768]{1,0:T(8,128)S(1)}, f32[64,768]{1,0:T(8,128)S(1)}, u32[]{:S(2)}, u32[]{:S(2)}) collective-permute-start(f32[64,768]{1,0:T(8,128)S(1)} %shard_map.58.own), channel_id=1, source_target_pairs={{0,1},{1,0},{2,3},{3,2},{4,5},{5,4},{6,7},{7,6},{8,9},{9,8},{10,11... | collective-permute-start | bytes 589832 | tf_op jit(solution)/shard_map/ppermute | solution.py:256
  93.7 0.4 shard_map.59.own_terms
  94.1 1.0 collective-permute-done.3.other
  95.1 0.5 shard_map.60
  95.6 9.0 %all_to_all.45 = f32[8,9,4,128]{3,2,1,0:T(4,128)S(1)} all-to-all(f32[8,9,4,128]{3,2,1,0:T(4,128)S(1)} %shard_map.60), channel_id=1, replica_groups={{256,0,128,384,264,8,136,392},{272,16,144,400,280,24,152,408},{288,32,1..., dimensions={0} | all-to-all | bytes 294912 | tf_op jit(solution)/shard_map/all_to_all | solution.py:247
  104.7 17.3 %all_to_all.46 = f32[8,9,4,128]{3,2,1,0:T(4,128)S(1)} all-to-all(f32[8,9,4,128]{3,2,1,0:T(4,128)S(1)} %broadcast_in_dim.22), channel_id=1, replica_groups={{72,0,88,16,104,32,120,48},{64,8,80,24,96,40,112,56},{200,128,216,144,2..., dimensions={0} | all-to-all | bytes 294912 | tf_op jit(solution)/shard_map/all_to_all | solution.py:247
  122.0 8.9 %all_to_all.47.sums = f32[8,9,4,128]{3,2,1,0:T(4,128)S(1)} all-to-all(f32[8,9,4,128]{3,2,1,0:T(4,128)S(1)} %broadcast_in_dim.23), channel_id=1, replica_groups={{256,0,128,384,264,8,136,392},{272,16,144,400,280,24,152,408},{288,32,1..., dimensions={0} | all-to-all | bytes 294912 | tf_op jit(solution)/shard_map/all_to_all | solution.py:247
  130.9 1.6 %shard_map.61 = (f32[64,1536]{1,0:T(8,128)}, f32[64,512]{1,0:T(8,128)}) custom-call(s32[1]{0:T(128)} %bitcast.core, f32[8,9,4,128]{3,2,1,0:T(4,128)S(1)} %all_to_all.47.sums, f32[64,512]{1,0:T(8,128)S(1)} %get-tuple-element.8.spec.old, f32[64,768]{1,0:T(8,128)S(1)} %shard_map.58.own, f32[64,768]{1,0:T(8,128)S(1)} %collective-permute-done.3.other), custom_call_target="tpu_custom_call" | custom-call | flops 200000000 | bytes 2000000 | tf_op jit(solution)/shard_map/pallas_call | solution.py:233
  (10 shorter events, 0.3 us)
Async XLA Ops:
  0.6 0.9 copy-start.1
  1.5 1.4 %copy-start = (bf16[1536,512]{1,0:T(8,128)(2,1)S(1)}, bf16[1536,512]{1,0:T(8,128)(2,1)}, u32[]{:S(2)}) copy-start(bf16[1536,512]{1,0:T(8,128)(2,1)} %data.15) | copy-start | bytes 4718596
  1.9 3.4 %copy-start.2 = (f32[64,512]{1,0:T(8,128)S(1)}, f32[64,512]{1,0:T(8,128)}, u32[]{:S(2)}) copy-start(f32[64,512]{1,0:T(8,128)} %old.3) | copy-start | bytes 393220
  3.3 3.4 %collective-permute-start = (f32[52,8,128]{2,1,0:T(8,128)S(1)}, f32[52,8,128]{2,1,0:T(8,128)S(1)}, u32[]{:S(2)}, u32[]{:S(2)}) collective-permute-start(f32[52,8,128]{2,1,0:T(8,128)S(1)} %shard_map.51.send), channel_id=1, source_target_pairs={{0,1},{1,0},{2,3},{3,2},{4,5},{5,4},{6,7},{7,6},{8,9},{9,8},{10,11... | collective-permute-start | bytes 638984 | tf_op jit(solution)/shard_map/ppermute | solution.py:256
  5.6 20.8 %copy-start.3 = (f32[64,1536]{1,0:T(8,128)S(1)}, f32[64,1536]{1,0:T(8,128)}, u32[]{:S(2)}) copy-start(f32[64,1536]{1,0:T(8,128)} %old.2) | copy-start | bytes 1179652
  27.4 3.3 %collective-permute-start.1 = (f32[64,768]{1,0:T(8,128)S(1)}, f32[64,768]{1,0:T(8,128)S(1)}, u32[]{:S(2)}, u32[]{:S(2)}) collective-permute-start(f32[64,768]{1,0:T(8,128)S(1)} %shard_map.53.own.old), channel_id=1, source_target_pairs={{0,1},{1,0},{2,3},{3,2},{4,5},{5,4},{6,7},{7,6},{8,9},{9,8},{10,11... | collective-permute-start | bytes 589832 | tf_op jit(solution)/shard_map/ppermute | solution.py:256
  71.3 3.4 %collective-permute-start.2 = (f32[52,8,128]{2,1,0:T(8,128)S(1)}, f32[52,8,128]{2,1,0:T(8,128)S(1)}, u32[]{:S(2)}, u32[]{:S(2)}) collective-permute-start(f32[52,8,128]{2,1,0:T(8,128)S(1)} %get-tuple-element.9.send), channel_id=1, source_target_pairs={{0,1},{1,0},{2,3},{3,2},{4,5},{5,4},{6,7},{7,6},{8,9},{9,8},{10,11... | collective-permute-start | bytes 638984 | tf_op jit(solution)/shard_map/ppermute | solution.py:256
  91.8 3.3 %collective-permute-start.3 = (f32[64,768]{1,0:T(8,128)S(1)}, f32[64,768]{1,0:T(8,128)S(1)}, u32[]{:S(2)}, u32[]{:S(2)}) collective-permute-start(f32[64,768]{1,0:T(8,128)S(1)} %shard_map.58.own), channel_id=1, source_target_pairs={{0,1},{1,0},{2,3},{3,2},{4,5},{5,4},{6,7},{7,6},{8,9},{9,8},{10,11... | collective-permute-start | bytes 589832 | tf_op jit(solution)/shard_map/ppermute | solution.py:256

commit v6 on v5

--- a/solution.py
+++ b/solution.py
@@ -18,7 +18,7 @@
 
 
 FROM_MIDDLE = (2, 0, 1, 3)
-PAIRS_FROM_MIDDLE = (4, 0, 5, 1, 6, 2, 7, 3)
+PAIRS_FROM_MIDDLE = (4, 0, 1, 7, 2, 6, 3, 5)
 NEAR = [[holder(x, pair, low) for low in range(2) for x in FROM_MIDDLE] for pair in range(8)]
 FAR = [[holder(x, pair, low) for pair in PAIRS_FROM_MIDDLE] for x in range(4) for low in range(2)]
 COLUMN = [[y * 2 for y in FROM_MIDDLE], [y * 2 + 1 for y in (2, 0, 3, 1)]]

time: 134 us -> 134 us (level)
  no operation moved by 1% of the time
where the time goes in v6:
time: 134 us; the launch traced here: 133 us
  blocking collectives  110 us (82%)
  Pallas kernels  8.11 us (6%)
  starting transfers between devices  7.73 us (6%)
  waiting for transfers between devices  4.07 us (3%)
  local copies, waits for them, and re-layouts  2.18 us (2%)
    all_to_all x8, blocking collectives, exchange(): return lax.all_to_all(parts, axis, 0, 0, axis_index_groups=groups)  110 us
    pallas_call x12, Pallas kernels, call(): pl.pallas_call(kernel, out_shape=outs, in_specs=specs, out_specs=jax.tree...  8.11 us
    ppermute x4, starting transfers between devices, swap(): return lax.ppermute(half, 'mass', SIBLING)  7.73 us
    ppermute x4, waiting for transfers between devices, swap(): return lax.ppermute(half, 'mass', SIBLING)  4.07 us
  transfers between devices with their start and end apart: 4, of which 4 were waited for; matrix products, arithmetic and copies ran while one was open for 0% of the time, Pallas kernels for 1%

profile of v6, /device:TPU:24, one launch (start us, length us, event | category | flops | bytes accessed | tf_op | source)
XLA Modules:
  0.0 132.6 jit_solution(8663132102690072647)
XLA Ops:
  0.6 0.0 copy-start.1
  0.6 0.9 copy-done.1
  1.5 0.0 copy-start
  1.5 0.3 shard_map.50
  1.9 0.0 copy-start.2
  1.9 1.1 copy-done
  2.9 0.3 shard_map.51.send
  3.3 1.9 %collective-permute-start = (f32[52,8,128]{2,1,0:T(8,128)S(1)}, f32[52,8,128]{2,1,0:T(8,128)S(1)}, u32[]{:S(2)}, u32[]{:S(2)}) collective-permute-start(f32[52,8,128]{2,1,0:T(8,128)S(1)} %shard_map.51.send), channel_id=1, source_target_pairs={{0,1},{1,0},{2,3},{3,2},{4,5},{5,4},{6,7},{7,6},{8,9},{9,8},{10,11... | collective-permute-start | bytes 638984 | tf_op jit(solution)/shard_map/ppermute | solution.py:256
  5.2 0.0 copy-done.2
  5.2 0.3 shard_map.52
  5.6 0.0 copy-start.3
  5.6 1.1 collective-permute-done
  6.7 0.1 broadcast_in_dim.18
  6.8 19.6 %all_to_all.40.parts = f32[4,52,8,128]{3,2,1,0:T(8,128)S(1)} all-to-all(f32[4,52,8,128]{3,2,1,0:T(8,128)S(1)} %broadcast_in_dim.18), channel_id=1, replica_groups={{4,0,2,6},{5,1,7,3},{12,8,10,14},{13,9,15,11},{20,16,18,22},{21,17,23,1..., dimensions={0} | all-to-all | bytes 1703936 | tf_op jit(solution)/shard_map/all_to_all | solution.py:247
  26.4 0.0 copy-done.3
  26.4 1.0 shard_map.53.own.old
  27.4 1.9 %collective-permute-start.1 = (f32[64,768]{1,0:T(8,128)S(1)}, f32[64,768]{1,0:T(8,128)S(1)}, u32[]{:S(2)}, u32[]{:S(2)}) collective-permute-start(f32[64,768]{1,0:T(8,128)S(1)} %shard_map.53.own.old), channel_id=1, source_target_pairs={{0,1},{1,0},{2,3},{3,2},{4,5},{5,4},{6,7},{7,6},{8,9},{9,8},{10,11... | collective-permute-start | bytes 589832 | tf_op jit(solution)/shard_map/ppermute | solution.py:256
  29.3 0.4 shard_map.54.own_terms
  29.7 1.0 collective-permute-done.1.other
  30.7 0.5 shard_map.55
  31.2 8.6 %all_to_all.41 = f32[8,9,4,128]{3,2,1,0:T(4,128)S(1)} all-to-all(f32[8,9,4,128]{3,2,1,0:T(4,128)S(1)} %shard_map.55), channel_id=1, replica_groups={{256,0,128,384,264,8,136,392},{272,16,144,400,280,24,152,408},{288,32,1..., dimensions={0} | all-to-all | bytes 294912 | tf_op jit(solution)/shard_map/all_to_all | solution.py:247
  39.9 21.1 %all_to_all.42 = f32[8,9,4,128]{3,2,1,0:T(4,128)S(1)} all-to-all(f32[8,9,4,128]{3,2,1,0:T(4,128)S(1)} %broadcast_in_dim.19), channel_id=1, replica_groups={{72,0,16,120,32,104,48,88},{64,8,24,112,40,96,56,80},{200,128,144,248,1..., dimensions={0} | all-to-all | bytes 294912 | tf_op jit(solution)/shard_map/all_to_all | solution.py:247
  61.0 8.8 %all_to_all.43.sums = f32[8,9,4,128]{3,2,1,0:T(4,128)S(1)} all-to-all(f32[8,9,4,128]{3,2,1,0:T(4,128)S(1)} %broadcast_in_dim.20), channel_id=1, replica_groups={{256,0,128,384,264,8,136,392},{272,16,144,400,280,24,152,408},{288,32,1..., dimensions={0} | all-to-all | bytes 294912 | tf_op jit(solution)/shard_map/all_to_all | solution.py:247
  69.8 1.3 shard_map.56
  71.1 2.0 %collective-permute-start.2 = (f32[52,8,128]{2,1,0:T(8,128)S(1)}, f32[52,8,128]{2,1,0:T(8,128)S(1)}, u32[]{:S(2)}, u32[]{:S(2)}) collective-permute-start(f32[52,8,128]{2,1,0:T(8,128)S(1)} %get-tuple-element.9.send), channel_id=1, source_target_pairs={{0,1},{1,0},{2,3},{3,2},{4,5},{5,4},{6,7},{7,6},{8,9},{9,8},{10,11... | collective-permute-start | bytes 638984 | tf_op jit(solution)/shard_map/ppermute | solution.py:256
  73.1 0.3 shard_map.57
  73.4 1.1 collective-permute-done.2
  74.5 0.1 broadcast_in_dim.21
  74.6 16.0 %all_to_all.44.parts = f32[4,52,8,128]{3,2,1,0:T(8,128)S(1)} all-to-all(f32[4,52,8,128]{3,2,1,0:T(8,128)S(1)} %broadcast_in_dim.21), channel_id=1, replica_groups={{4,0,2,6},{5,1,7,3},{12,8,10,14},{13,9,15,11},{20,16,18,22},{21,17,23,1..., dimensions={0} | all-to-all | bytes 1703936 | tf_op jit(solution)/shard_map/all_to_all | solution.py:247
  90.5 1.0 shard_map.58.own
  91.6 1.9 %collective-permute-start.3 = (f32[64,768]{1,0:T(8,128)S(1)}, f32[64,768]{1,0:T(8,128)S(1)}, u32[]{:S(2)}, u32[]{:S(2)}) collective-permute-start(f32[64,768]{1,0:T(8,128)S(1)} %shard_map.58.own), channel_id=1, source_target_pairs={{0,1},{1,0},{2,3},{3,2},{4,5},{5,4},{6,7},{7,6},{8,9},{9,8},{10,11... | collective-permute-start | bytes 589832 | tf_op jit(solution)/shard_map/ppermute | solution.py:256
  93.5 0.4 shard_map.59.own_terms
  93.9 1.0 collective-permute-done.3.other
  94.9 0.5 shard_map.60
  95.4 9.0 %all_to_all.45 = f32[8,9,4,128]{3,2,1,0:T(4,128)S(1)} all-to-all(f32[8,9,4,128]{3,2,1,0:T(4,128)S(1)} %shard_map.60), channel_id=1, replica_groups={{256,0,128,384,264,8,136,392},{272,16,144,400,280,24,152,408},{288,32,1..., dimensions={0} | all-to-all | bytes 294912 | tf_op jit(solution)/shard_map/all_to_all | solution.py:247
  104.5 17.6 %all_to_all.46 = f32[8,9,4,128]{3,2,1,0:T(4,128)S(1)} all-to-all(f32[8,9,4,128]{3,2,1,0:T(4,128)S(1)} %broadcast_in_dim.22), channel_id=1, replica_groups={{72,0,16,120,32,104,48,88},{64,8,24,112,40,96,56,80},{200,128,144,248,1..., dimensions={0} | all-to-all | bytes 294912 | tf_op jit(solution)/shard_map/all_to_all | solution.py:247
  122.1 9.0 %all_to_all.47.sums = f32[8,9,4,128]{3,2,1,0:T(4,128)S(1)} all-to-all(f32[8,9,4,128]{3,2,1,0:T(4,128)S(1)} %broadcast_in_dim.23), channel_id=1, replica_groups={{256,0,128,384,264,8,136,392},{272,16,144,400,280,24,152,408},{288,32,1..., dimensions={0} | all-to-all | bytes 294912 | tf_op jit(solution)/shard_map/all_to_all | solution.py:247
  131.1 1.6 %shard_map.61 = (f32[64,1536]{1,0:T(8,128)}, f32[64,512]{1,0:T(8,128)}) custom-call(s32[1]{0:T(128)} %bitcast.core, f32[8,9,4,128]{3,2,1,0:T(4,128)S(1)} %all_to_all.47.sums, f32[64,512]{1,0:T(8,128)S(1)} %get-tuple-element.8.spec.old, f32[64,768]{1,0:T(8,128)S(1)} %shard_map.58.own, f32[64,768]{1,0:T(8,128)S(1)} %collective-permute-done.3.other), custom_call_target="tpu_custom_call" | custom-call | flops 200000000 | bytes 2000000 | tf_op jit(solution)/shard_map/pallas_call | solution.py:233
  (10 shorter events, 0.3 us)
Async XLA Ops:
  0.6 0.9 copy-start.1
  1.5 1.4 %copy-start = (bf16[1536,512]{1,0:T(8,128)(2,1)S(1)}, bf16[1536,512]{1,0:T(8,128)(2,1)}, u32[]{:S(2)}) copy-start(bf16[1536,512]{1,0:T(8,128)(2,1)} %data.15) | copy-start | bytes 4718596
  1.9 3.4 %copy-start.2 = (f32[64,512]{1,0:T(8,128)S(1)}, f32[64,512]{1,0:T(8,128)}, u32[]{:S(2)}) copy-start(f32[64,512]{1,0:T(8,128)} %old.3) | copy-start | bytes 393220
  3.3 3.4 %collective-permute-start = (f32[52,8,128]{2,1,0:T(8,128)S(1)}, f32[52,8,128]{2,1,0:T(8,128)S(1)}, u32[]{:S(2)}, u32[]{:S(2)}) collective-permute-start(f32[52,8,128]{2,1,0:T(8,128)S(1)} %shard_map.51.send), channel_id=1, source_target_pairs={{0,1},{1,0},{2,3},{3,2},{4,5},{5,4},{6,7},{7,6},{8,9},{9,8},{10,11... | collective-permute-start | bytes 638984 | tf_op jit(solution)/shard_map/ppermute | solution.py:256
  5.6 20.8 %copy-start.3 = (f32[64,1536]{1,0:T(8,128)S(1)}, f32[64,1536]{1,0:T(8,128)}, u32[]{:S(2)}) copy-start(f32[64,1536]{1,0:T(8,128)} %old.2) | copy-start | bytes 1179652
  27.4 3.3 %collective-permute-start.1 = (f32[64,768]{1,0:T(8,128)S(1)}, f32[64,768]{1,0:T(8,128)S(1)}, u32[]{:S(2)}, u32[]{:S(2)}) collective-permute-start(f32[64,768]{1,0:T(8,128)S(1)} %shard_map.53.own.old), channel_id=1, source_target_pairs={{0,1},{1,0},{2,3},{3,2},{4,5},{5,4},{6,7},{7,6},{8,9},{9,8},{10,11... | collective-permute-start | bytes 589832 | tf_op jit(solution)/shard_map/ppermute | solution.py:256
  71.1 3.4 %collective-permute-start.2 = (f32[52,8,128]{2,1,0:T(8,128)S(1)}, f32[52,8,128]{2,1,0:T(8,128)S(1)}, u32[]{:S(2)}, u32[]{:S(2)}) collective-permute-start(f32[52,8,128]{2,1,0:T(8,128)S(1)} %get-tuple-element.9.send), channel_id=1, source_target_pairs={{0,1},{1,0},{2,3},{3,2},{4,5},{5,4},{6,7},{7,6},{8,9},{9,8},{10,11... | collective-permute-start | bytes 638984 | tf_op jit(solution)/shard_map/ppermute | solution.py:256
  91.6 3.3 %collective-permute-start.3 = (f32[64,768]{1,0:T(8,128)S(1)}, f32[64,768]{1,0:T(8,128)S(1)}, u32[]{:S(2)}, u32[]{:S(2)}) collective-permute-start(f32[64,768]{1,0:T(8,128)S(1)} %shard_map.58.own), channel_id=1, source_target_pairs={{0,1},{1,0},{2,3},{3,2},{4,5},{5,4},{6,7},{7,6},{8,9},{9,8},{10,11... | collective-permute-start | bytes 589832 | tf_op jit(solution)/shard_map/ppermute | solution.py:256
